TPU v7x, 32 devices: a whole 2x2x4 slice. The times are simulated.
32 devices in a mesh: ctx: 4 (over y, x), exp: 4 (over z), rep: 2 (over core).
Axes of the slice: x: 2, y: 2, z: 4, core: 2. Of those that a mesh axis runs over, the one named last changes fastest.
Arguments:
- tokens: bfloat16 [1024, 7168], P(('rep', 'exp'), 'ctx'), parts along dimension 0, may hold values from -6 to 6
- routes: int32 [1024, 2], P(('rep', 'exp')), parts along dimension 0, may hold values from 0 to 3, all different within a row; in each aligned block of 128 rows (0 to 127, 128 to 255, ...) at most 80 rows name the same one
- event_weights: float32 [1024, 2], P(('rep', 'exp')), parts along dimension 0, may hold values from 0.25 to 2
- cotangent: bfloat16 [512, 7168], P('exp', 'ctx'), may hold values from -0.59765625 to 0.59765625
- w_gate: bfloat16 [4, 7168, 1024], P('exp', 'ctx'), may hold values from -0.0625 to 0.0625
- w_up: bfloat16 [4, 7168, 1024], P('exp', 'ctx'), may hold values from -0.0625 to 0.0625
- w_down: bfloat16 [4, 1024, 7168], P('exp', None, 'ctx'), may hold values from -0.1875 to 0.1875
Outputs:
- mixed: bfloat16 [1024, 7168], P(('rep', 'exp'), 'ctx'), parts along dimension 0
- token_grad: bfloat16 [1024, 7168], P(('rep', 'exp'), 'ctx'), parts along dimension 0
- weight_grad: float32 [1024, 2], P(('rep', 'exp')), parts along dimension 0
There are 2 independent parts, one for each index of `rep`. A program takes and returns all parts, laid end to end along the dimension named above; an argument that names none is the same for every part. Nothing has to cross between parts.
Inputs may be any that keep to these rules, and one draw needn't show every extreme that they name: `routes`: each token names 2 different experts. Among the 128 tokens of one index of exp (aligned blocks of 128 rows) no expert is named more than 80 times, a bound that some block reaches; every expert is named somewhere.
All inputs are finite; a program needn't handle non-finite values.
Results may differ from a plain program's by a relative error of at most 0.03.
Values may be sent and summed in bfloat16 or wider, within the bound.
A program may use at most 64 MiB of HBM per device.

v0:
```python
import jax
import jax.numpy as jnp
from jax import lax
from jax.sharding import PartitionSpec as P


def activate(gate_pre, up_pre, back_pre):
    squash = jax.nn.sigmoid(gate_pre)
    hidden_act = (gate_pre * squash * up_pre).astype(jnp.bfloat16)
    grad_gate = (back_pre * up_pre * squash * (1.0 + gate_pre * (1.0 - squash))).astype(
        jnp.bfloat16
    )
    grad_up = (back_pre * gate_pre * squash).astype(jnp.bfloat16)
    return (hidden_act, grad_gate, grad_up)


def shards(tokens, routes, event_weights, cotangent, w_gate, w_up, w_down):
    owners = lax.axis_size("exp")
    owned, columns, hidden = w_gate.shape
    experts = owned * owners
    rows_here, fanout = routes.shape
    capacity = max(2, 5 * rows_here * fanout // (4 * experts))
    slot_count = owners * capacity
    routes_flat = routes.reshape(-1)
    onehot = (routes_flat[:, None] == jnp.arange(experts, dtype=jnp.int32)[None, :]).astype(
        jnp.int32
    )
    places = jnp.sum((jnp.cumsum(onehot, axis=0) - onehot) * onehot, axis=1)
    targets = routes_flat * capacity + places
    token_rows = jnp.repeat(tokens, fanout, axis=0)
    cot_rows = (
        event_weights.reshape(-1, 1) * jnp.repeat(cotangent.astype(jnp.float32), fanout, axis=0)
    ).astype(jnp.bfloat16)
    send_tokens = jnp.zeros((experts * capacity, columns), jnp.bfloat16).at[targets].set(token_rows)
    send_cots = jnp.zeros((experts * capacity, columns), jnp.bfloat16).at[targets].set(cot_rows)
    send_tokens = send_tokens.reshape(owners, owned * capacity, columns)
    send_cots = send_cots.reshape(owners, owned * capacity, columns)
    recv_tokens, recv_cots = (
        lax.all_to_all(send_tokens, "exp", split_axis=0, concat_axis=0, tiled=True),
        lax.all_to_all(send_cots, "exp", split_axis=0, concat_axis=0, tiled=True),
    )

    def arrange(buffer):
        return (
            buffer.reshape(owners, owned, capacity, columns)
            .transpose(1, 0, 2, 3)
            .reshape(owned, slot_count, columns)
        )

    expert_in = arrange(recv_tokens)
    expert_cot = arrange(recv_cots)
    shares = lax.psum_scatter(
        jnp.stack(
            [
                jnp.einsum("jsd,jdf->fjs", expert_in, w_gate, preferred_element_type=jnp.float32),
                jnp.einsum("jsd,jdf->fjs", expert_in, w_up, preferred_element_type=jnp.float32),
                jnp.einsum("jsd,jfd->fjs", expert_cot, w_down, preferred_element_type=jnp.float32),
            ],
            axis=1,
        ).astype(jnp.bfloat16),
        "ctx",
        scatter_dimension=0,
        tiled=True,
    ).astype(jnp.float32)
    hidden_share, gate_share, up_share = activate(shares[:, 0], shares[:, 1], shares[:, 2])
    hidden_act, grad_gate, grad_up = (
        lax.all_gather(hidden_share, "ctx", axis=0, tiled=True),
        lax.all_gather(gate_share, "ctx", axis=0, tiled=True),
        lax.all_gather(up_share, "ctx", axis=0, tiled=True),
    )
    expert_out = jnp.einsum(
        "fjs,jfd->jsd", hidden_act, w_down, preferred_element_type=jnp.float32
    ).astype(jnp.bfloat16)
    event_grad = (
        jnp.einsum("fjs,jdf->jsd", grad_gate, w_gate, preferred_element_type=jnp.float32)
        + jnp.einsum("fjs,jdf->jsd", grad_up, w_up, preferred_element_type=jnp.float32)
    ).astype(jnp.bfloat16)

    def restore(buffer):
        return (
            buffer.reshape(owned, owners, capacity, columns)
            .transpose(1, 0, 2, 3)
            .reshape(owners, owned * capacity, columns)
        )

    back_out, back_grad = (
        lax.all_to_all(restore(expert_out), "exp", split_axis=0, concat_axis=0, tiled=True),
        lax.all_to_all(restore(event_grad), "exp", split_axis=0, concat_axis=0, tiled=True),
    )
    out_rows = (
        back_out.reshape(experts * capacity, columns)[targets]
        .reshape(rows_here, fanout, columns)
        .astype(jnp.float32)
    )
    grad_rows = (
        back_grad.reshape(experts * capacity, columns)[targets]
        .reshape(rows_here, fanout, columns)
        .astype(jnp.float32)
    )
    mixed = jnp.sum(event_weights[:, :, None] * out_rows, axis=1).astype(jnp.bfloat16)
    token_grad = jnp.sum(grad_rows, axis=1).astype(jnp.bfloat16)
    weight_part = jnp.einsum("td,tkd->tk", cotangent.astype(jnp.float32), out_rows)
    weight_grad = lax.psum(weight_part, "ctx")
    return (mixed, token_grad, weight_grad)


def solution(mesh):
    in_specs = (
        P(("rep", "exp"), "ctx"),
        P(("rep", "exp"), None),
        P(("rep", "exp"), None),
        P("exp", "ctx"),
        P("exp", "ctx", None),
        P("exp", "ctx", None),
        P("exp", None, "ctx"),
    )
    out_specs = (P(("rep", "exp"), "ctx"), P(("rep", "exp"), "ctx"), P(("rep", "exp"), None))
    return jax.shard_map(shards, mesh=mesh, in_specs=in_specs, out_specs=out_specs, check_vma=False)
```

profile of v0, /device:TPU:0, one launch (start us, length us, event | category | flops | bytes accessed | tf_op | source)
XLA Modules:
  0.0 235.0 jit_solution(12355715797418645496)
XLA Ops:
  7.2 0.8 copy.15
  8.0 0.1 eq.29
  8.1 0.1 eq.25
  8.2 0.7 broadcast_multiply_fusion
  8.9 1.2 reduce-window.6
  10.1 0.1 slice.24
  10.2 0.1 copy.17
  10.4 0.1 copy.18
  10.4 0.1 add_bitcast_fusion
  10.5 0.1 copy.14
  10.6 0.1 mul.128
  10.8 1.5 broadcast_in_dim.4
  12.3 0.3 reshape.356
  12.6 0.0 copy-start.3
  12.6 0.0 copy-start.1
  12.7 3.0 %scatter_custom_fusion = bf16[320,1792]{1,0:T(8,128)(2,1)} fusion(s32[256]{0:T(256)S(1)} %bitcast.116, bf16[256,1792]{1,0:T(8,128)(2,1)S(1)} %reshape.356, bf16[]{:T(256)} %constant.6.clone.1), kind=kCustom, calls=%fused_computation.36 | custom fusion | bytes 1146882 | tf_op jit(solution)/shard_map/scatter | solution.py:34
  15.7 6.3 %all-to-all-start = ((bf16[4,80,1792]{2,1,0:T(8,128)(2,1)}), bf16[4,80,1792]{2,1,0:T(8,128)(2,1)S(1)}, u32[]{:S(2)}, u32[]{:S(2)}) async-start(bf16[4,80,1792]{2,1,0:T(8,128)(2,1)} %bitcast.4), calls=%async_computation | async-start | bytes 2293760 | tf_op jit(solution)/shard_map/all_to_all | solution.py:39
  22.1 0.0 copy-done.3
  22.1 0.1 copy.13
  22.2 0.1 mul.130
  22.3 0.0 copy-done.1
  22.3 1.7 broadcast_in_dim.5
  24.0 2.5 %reshape.325 = f32[256,1792]{1,0:T(8,128)S(1)} reshape(f32[128,2,1792]{2,1,0:T(2,128)} %broadcast_in_dim.5) | data formatting | bytes 3670016 | tf_op jit(solution)/shard_map/reshape | solution.py:32
  26.6 3.1 %scatter_custom_fusion.1 = bf16[320,1792]{1,0:T(8,128)(2,1)} fusion(s32[256]{0:T(256)S(1)} %bitcast.117, f32[256,1792]{1,0:T(8,128)S(1)} %reshape.325, f32[256]{0:T(256)S(1)} %mul.130, bf16[]{:T(256)} %constant.6.clone.1), kind=kCustom, calls=%fused_computation.28 | custom fusion | flops 917504 | bytes 2982914 | tf_op jit(solution)/shard_map/scatter | solution.py:35
  29.7 20.2 %all-to-all-done = bf16[4,80,1792]{2,1,0:T(8,128)(2,1)S(1)} async-done(((bf16[4,80,1792]{2,1,0:T(8,128)(2,1)}), bf16[4,80,1792]{2,1,0:T(8,128)(2,1)S(1)}, u32[]{:S(2)}, u32[]{:S(2)}) %all-to-all-start) | async-done | bytes 1146912 | tf_op jit(solution)/shard_map/all_to_all | solution.py:39
  49.9 3.5 %all-to-all-start.1 = ((bf16[4,80,1792]{2,1,0:T(8,128)(2,1)}), bf16[4,80,1792]{2,1,0:T(8,128)(2,1)S(1)}, u32[]{:S(2)}, u32[]{:S(2)}) async-start(bf16[4,80,1792]{2,1,0:T(8,128)(2,1)} %bitcast.12), calls=%async_computation.1 | async-start | bytes 2293760 | tf_op jit(solution)/shard_map/all_to_all | solution.py:40
  53.4 0.0 reduce-scatter.2.cloned.1.call-start
  53.5 0.0 copy-start.5
  53.5 3.6 %fusion.33 = bf16[1024,1,1,320]{0,3,2,1:T(8,128)(2,1)S(1)} fusion(bf16[320,1792]{1,0:T(8,128)(2,1)S(1)} %bitcast.111, bf16[1,1792,1024]{2,1,0:T(8,128)(2,1)} %param.12), kind=kOutput, calls=%fused_computation.26 | convolution fusion | flops 1174732800 | bytes 5472256 | tf_op jit(solution)/shard_map/jsd,jdf->fjs/dot_general | solution.py:56
  57.1 0.0 copy-done.5
  57.1 2.3 fusion.36
  59.3 21.4 %all-to-all-done.1 = bf16[4,80,1792]{2,1,0:T(8,128)(2,1)S(1)} async-done(((bf16[4,80,1792]{2,1,0:T(8,128)(2,1)}), bf16[4,80,1792]{2,1,0:T(8,128)(2,1)S(1)}, u32[]{:S(2)}, u32[]{:S(2)}) %all-to-all-start.1) | async-done | bytes 1146912 | tf_op jit(solution)/shard_map/all_to_all | solution.py:40
  80.7 0.0 copy-start
  80.7 3.5 %fusion.30 = bf16[1024,1,1,320]{0,3,2,1:T(8,128)(2,1)S(1)} fusion(bf16[320,1792]{1,0:T(8,128)(2,1)S(1)} %bitcast.113, bf16[1,1024,1792]{2,1,0:T(8,128)(2,1)} %param.13), kind=kOutput, calls=%fused_computation.25 | convolution fusion | flops 1174732800 | bytes 5472256 | tf_op jit(solution)/shard_map/jsd,jfd->fjs/dot_general | solution.py:57
  84.2 0.0 copy-done
  84.2 1.5 pad_maximum_fusion
  85.7 0.0 reduce-scatter.2.cloned.1.call-update
  85.8 33.4 %reduce-scatter.2.cloned.1.call-done = bf16[256,3,1,320]{0,3,2,1:T(8,128)(2,1)} async-done(((bf16[1024,3,1,320]{0,3,2,1:T(8,128)(2,1)}), bf16[256,3,1,320]{0,3,2,1:T(8,128)(2,1)}) %reduce-scatter.2.cloned.1.call-update) | async-done | bytes 491536 | tf_op jit(solution)/shard_map/reduce_scatter | solution.py:52
  119.1 0.0 copy-start.4
  119.1 1.3 convert_element_type.79
  120.4 0.2 multiply_convert_fusion.3
  120.6 15.7 %all_gather.11 = bf16[1024,1,320]{0,2,1:T(8,128)(2,1)S(1)} all-gather(bf16[256,1,320]{0,2,1:T(8,128)(2,1)S(1)} %get-tuple-element.4), channel_id=1, replica_groups=mesh['ctx'=4,'exp'=4,'rep'=2] {'ctx'}, dimensions={0}, use_global_device_ids=true | all-gather | bytes 819200 | tf_op jit(solution)/shard_map/all_gather | solution.py:69
  136.3 0.0 copy-done.4
  136.3 1.4 fusion.4
  137.7 12.3 %all_gather.10 = bf16[1024,1,320]{0,2,1:T(8,128)(2,1)S(1)} all-gather(bf16[256,1,320]{0,2,1:T(8,128)(2,1)S(1)} %get-tuple-element.3), channel_id=1, replica_groups=mesh['ctx'=4,'exp'=4,'rep'=2] {'ctx'}, dimensions={0}, use_global_device_ids=true | all-gather | bytes 819200 | tf_op jit(solution)/shard_map/all_gather | solution.py:68
  150.0 0.0 copy-done.6
  150.0 2.5 %fusion.15 = bf16[320,1792]{1,0:T(8,128)(2,1)} fusion(f32[320,1792]{1,0:T(8,128)S(1)} %fusion.4, bf16[1,1792,1024]{2,1,0:T(8,128)(2,1)S(1)} %copy-done.6, bf16[1024,1,320]{0,2,1:T(8,128)(2,1)S(1)} %all_gather.10), kind=kOutput, calls=%fused_computation.17 | convolution fusion | flops 1175552000 | bytes 7766016 | tf_op jit(solution)/shard_map/fjs,jdf->jsd/dot_general | solution.py:75
  152.5 4.6 %all-to-all-start.3 = ((bf16[4,80,1792]{2,1,0:T(8,128)(2,1)}), bf16[4,80,1792]{2,1,0:T(8,128)(2,1)S(1)}, u32[]{:S(2)}, u32[]{:S(2)}) async-start(bf16[4,80,1792]{2,1,0:T(8,128)(2,1)} %bitcast.25), calls=%async_computation.4 | async-start | bytes 2293760 | tf_op jit(solution)/shard_map/all_to_all | solution.py:88
  157.0 13.1 %all_gather.9 = bf16[1024,1,320]{0,2,1:T(8,128)(2,1)S(1)} all-gather(bf16[256,1,320]{0,2,1:T(8,128)(2,1)S(1)} %get-tuple-element.5), channel_id=1, replica_groups=mesh['ctx'=4,'exp'=4,'rep'=2] {'ctx'}, dimensions={0}, use_global_device_ids=true | all-gather | bytes 819200 | tf_op jit(solution)/shard_map/all_gather | solution.py:67
  170.2 4.4 %fusion.18 = bf16[320,1792]{1,0:T(8,128)(2,1)} fusion(bf16[1,1024,1792]{2,1,0:T(8,128)(2,1)} %param.13, bf16[1024,1,320]{0,2,1:T(8,128)(2,1)S(1)} %all_gather.9), kind=kOutput, calls=%fused_computation.18 | convolution fusion | flops 1174978560 | bytes 5472256 | tf_op jit(solution)/shard_map/fjs,jfd->jsd/dot_general | solution.py:71
  174.6 6.8 %all-to-all-done.3 = bf16[4,80,1792]{2,1,0:T(8,128)(2,1)S(1)} async-done(((bf16[4,80,1792]{2,1,0:T(8,128)(2,1)}), bf16[4,80,1792]{2,1,0:T(8,128)(2,1)S(1)}, u32[]{:S(2)}, u32[]{:S(2)}) %all-to-all-start.3) | async-done | bytes 1146912 | tf_op jit(solution)/shard_map/all_to_all | solution.py:88
  181.3 3.5 %all-to-all-start.2 = ((bf16[4,80,1792]{2,1,0:T(8,128)(2,1)}), bf16[4,80,1792]{2,1,0:T(8,128)(2,1)S(1)}, u32[]{:S(2)}, u32[]{:S(2)}) async-start(bf16[4,80,1792]{2,1,0:T(8,128)(2,1)} %bitcast.20), calls=%async_computation.3 | async-start | bytes 2293760 | tf_op jit(solution)/shard_map/all_to_all | solution.py:87
  184.9 1.3 gather_fusion.1
  186.2 0.3 reshape.335
  186.6 3.4 %reduce_sum.35 = bf16[128,1792]{1,0:T(8,128)(2,1)} reduce(bf16[128,2,1792]{2,1,0:T(2,128)(2,1)S(1)} %reshape.335, bf16[]{:T(256)} %constant.6.clone.1), dimensions={1}, to_apply=%region_7.8 | reduce | flops 229376 | bytes 1376258 | tf_op jit(solution)/shard_map/reduce_sum | solution.py:101
  190.0 21.3 %all-to-all-done.2 = bf16[4,80,1792]{2,1,0:T(8,128)(2,1)S(1)} async-done(((bf16[4,80,1792]{2,1,0:T(8,128)(2,1)}), bf16[4,80,1792]{2,1,0:T(8,128)(2,1)S(1)}, u32[]{:S(2)}, u32[]{:S(2)}) %all-to-all-start.2) | async-done | bytes 1146912 | tf_op jit(solution)/shard_map/all_to_all | solution.py:87
  211.3 1.3 gather_fusion
  212.6 0.0 copy-start.2
  212.6 0.3 reshape.331
  213.0 3.6 %multiply_reduce_fusion = bf16[128,1792]{1,0:T(8,128)(2,1)} fusion(bf16[128,2,1792]{2,1,0:T(2,128)(2,1)S(1)} %reshape.331, f32[128,2]{1,0:T(8,128)S(1)} %copy.13), kind=kLoop, calls=%fused_computation.20 | loop fusion | flops 1146880 | bytes 1377280 | tf_op jit(solution)/shard_map/reduce_sum | solution.py:100
  216.6 0.0 copy-done.2
  216.6 2.0 fusion.41
  218.6 0.1 copy.21
  218.7 9.5 %psum.7 = f32[128,2]{0,1:T(2,128)} all-reduce(f32[128,2]{0,1:T(2,128)S(1)} %bitcast.115), channel_id=1, replica_groups=mesh['ctx'=4,'exp'=4,'rep'=2] {'ctx'}, use_global_device_ids=true, to_apply=%region_8.9 | all-reduce | flops 256 | bytes 2048 | tf_op jit(solution)/shard_map/psum | solution.py:103
  (7 shorter events, 0.1 us)
Async XLA Ops:
  12.6 9.4 %copy-start.3 = (f32[128,2]{0,1:T(2,128)S(1)}, f32[128,2]{0,1:T(2,128)}, u32[]{:S(2)}) copy-start(f32[128,2]{0,1:T(2,128)} %param.9) | copy-start | bytes 3076
  12.6 9.7 %copy-start.1 = (bf16[128,1792]{1,0:T(8,128)(2,1)S(1)}, bf16[128,1792]{1,0:T(8,128)(2,1)}, u32[]{:S(2)}) copy-start(bf16[128,1792]{1,0:T(8,128)(2,1)} %param.10) | copy-start | bytes 1376260
  15.7 34.2 %all-to-all-start = ((bf16[4,80,1792]{2,1,0:T(8,128)(2,1)}), bf16[4,80,1792]{2,1,0:T(8,128)(2,1)S(1)}, u32[]{:S(2)}, u32[]{:S(2)}) async-start(bf16[4,80,1792]{2,1,0:T(8,128)(2,1)} %bitcast.4), calls=%async_computation | async-start | bytes 2293760 | tf_op jit(solution)/shard_map/all_to_all | solution.py:39
  49.9 30.8 %all-to-all-start.1 = ((bf16[4,80,1792]{2,1,0:T(8,128)(2,1)}), bf16[4,80,1792]{2,1,0:T(8,128)(2,1)S(1)}, u32[]{:S(2)}, u32[]{:S(2)}) async-start(bf16[4,80,1792]{2,1,0:T(8,128)(2,1)} %bitcast.12), calls=%async_computation.1 | async-start | bytes 2293760 | tf_op jit(solution)/shard_map/all_to_all | solution.py:40
  53.4 65.7 %reduce-scatter.2.cloned.1.call-start = ((), (), s32[]{:S(2)}) async-start(), calls=%async_computation.5 | async-start | bytes 2457600 | tf_op jit(solution)/shard_map/reduce_scatter | solution.py:52
  53.5 3.6 %copy-start.5 = (bf16[1,1792,1024]{2,1,0:T(8,128)(2,1)S(1)}, bf16[1,1792,1024]{2,1,0:T(8,128)(2,1)}, u32[]{:S(2)}) copy-start(bf16[1,1792,1024]{2,1,0:T(8,128)(2,1)} %param.11) | copy-start | bytes 11010052
  80.7 3.5 %copy-start = (bf16[1024,1,1,320]{0,3,2,1:T(8,128)(2,1)S(1)}, bf16[1024,1,1,320]{0,3,2,1:T(8,128)(2,1)}, u32[]{:S(2)}) copy-start(bf16[1024,1,1,320]{0,3,2,1:T(8,128)(2,1)} %fusion.36) | copy-start | bytes 1966084
  119.1 17.1 %copy-start.4 = (bf16[1,1792,1024]{2,1,0:T(8,128)(2,1)S(1)}, bf16[1,1792,1024]{2,1,0:T(8,128)(2,1)}, u32[]{:S(2)}) copy-start(bf16[1,1792,1024]{2,1,0:T(8,128)(2,1)} %param.12) | copy-start | bytes 11010052
  136.3 13.7 %copy-start.6 = (bf16[1,1792,1024]{2,1,0:T(8,128)(2,1)S(1)}, bf16[1,1792,1024]{2,1,0:T(8,128)(2,1)}, u32[]{:S(2)}) copy-start(bf16[1,1792,1024]{2,1,0:T(8,128)(2,1)} %param.11) | copy-start | bytes 11010052
  152.5 28.9 %all-to-all-start.3 = ((bf16[4,80,1792]{2,1,0:T(8,128)(2,1)}), bf16[4,80,1792]{2,1,0:T(8,128)(2,1)S(1)}, u32[]{:S(2)}, u32[]{:S(2)}) async-start(bf16[4,80,1792]{2,1,0:T(8,128)(2,1)} %bitcast.25), calls=%async_computation.4 | async-start | bytes 2293760 | tf_op jit(solution)/shard_map/all_to_all | solution.py:88
  181.3 29.9 %all-to-all-start.2 = ((bf16[4,80,1792]{2,1,0:T(8,128)(2,1)}), bf16[4,80,1792]{2,1,0:T(8,128)(2,1)S(1)}, u32[]{:S(2)}, u32[]{:S(2)}) async-start(bf16[4,80,1792]{2,1,0:T(8,128)(2,1)} %bitcast.20), calls=%async_computation.3 | async-start | bytes 2293760 | tf_op jit(solution)/shard_map/all_to_all | solution.py:87
  212.6 4.0 %copy-start.2 = (bf16[128,1792]{1,0:T(8,128)(2,1)S(1)}, bf16[128,1792]{1,0:T(8,128)(2,1)}, u32[]{:S(2)}) copy-start(bf16[128,1792]{1,0:T(8,128)(2,1)} %param.10) | copy-start | bytes 1376260
Sparse Core Ops, SparseCore 0:
  85.9 33.2 reduce-scatter.1
where the time goes:
time: 236 us; the launch traced here: 235 us
  waiting for transfers between devices  103 us (44%)
  blocking collectives  50.6 us (21%)
  matrix products  19.6 us (8%)
  starting transfers between devices  18 us (8%)
  other arithmetic  15 us (6%)
  local copies, waits for them, and re-layouts  14.5 us (6%)
  between operations  14.2 us (6%)
    reduce_scatter x1, waiting for transfers between devices, shards(): lax.psum_scatter(jnp.stack([jnp.einsum('jsd,jdf->fjs', expert_in, w_gate,...  33.4 us
    all_to_all x1, waiting for transfers between devices, shards(): lax.all_to_all(send_cots, 'exp', split_axis=0, concat_axis=0, tiled=True)  21.4 us
    all_to_all x1, waiting for transfers between devices, shards(): lax.all_to_all(restore(expert_out), 'exp', split_axis=0, concat_axis=0, t...  21.3 us
    all_to_all x1, waiting for transfers between devices, shards(): lax.all_to_all(send_tokens, 'exp', split_axis=0, concat_axis=0, tiled=True)  20.2 us
    all_gather x1, blocking collectives, shards(): lax.all_gather(up_share, 'ctx', axis=0, tiled=True)  15.7 us
    all_gather x1, blocking collectives, shards(): lax.all_gather(hidden_share, 'ctx', axis=0, tiled=True)  13.1 us
    all_gather x1, blocking collectives, shards(): lax.all_gather(gate_share, 'ctx', axis=0, tiled=True)  12.3 us
    psum x1, blocking collectives, shards(): weight_grad = lax.psum(weight_part, 'ctx')  9.48 us
  transfers between devices with their start and end apart: 5, of which 5 were waited for; matrix products, arithmetic and copies ran while one was open for 10% of the time, Pallas kernels for 0%

commit v1 on v0

--- a/solution.py
+++ b/solution.py
@@ -1,6 +1,10 @@
+import functools
+
 import jax
 import jax.numpy as jnp
 from jax import lax
+from jax.experimental import pallas as pl
+from jax.experimental.pallas import tpu as pltpu
 from jax.sharding import PartitionSpec as P
 
 
@@ -104,6 +108,413 @@
     return (mixed, token_grad, weight_grad)
 
 
+def fused(
+    sizes,
+    routes_ref, weights_ref, tokens_ref, cot_ref, gate_hbm, up_hbm, down_hbm,
+    mixed_ref, grad_ref, wgrad_ref,
+    gate_w, up_w, down_w, x_send, x_recv, rt_recv, cots, part, shares, acts, grads, saved,
+    out_send, out_recv, eg_send, eg_recv, wg_parts, mix_acc,
+    load_sem, x_ssem, x_rsem, rt_ssem, rt_rsem, far_up, far_down, far_rsem, sib_ssem, sib_rsem,
+    rs_ssem, rs_rsem, bk_ssem, bk_rsem, ag_ssem, ag_rsem, gg_ssem, gg_rsem,
+    out_ssem, out_rsem, eg_ssem, eg_rsem, wg_ssem, wg_rsem,
+):
+    owners, splits, capacity, rows, columns, hidden = sizes
+    part_f = hidden // splits
+    half = rows // 2
+    z, c, r = lax.axis_index("exp"), lax.axis_index("ctx"), lax.axis_index("rep")
+    bf, f32 = jnp.bfloat16, jnp.float32
+
+    def expert_at(d):
+        return lax.rem(z + d, owners)
+
+    def source_at(d):
+        return lax.rem(z - d + owners, owners)
+
+    def peer_at(q):
+        return lax.rem(c + q, splits)
+
+    def from_peer(q):
+        return lax.rem(c - q + splits, splits)
+
+    def remote(src, dst, ssem, rsem, **where):
+        return pltpu.make_async_remote_copy(
+            src_ref=src, dst_ref=dst, send_sem=ssem, recv_sem=rsem,
+            device_id=where, device_id_type=pl.DeviceIdType.MESH,
+        )
+
+    loads = [
+        pltpu.make_async_copy(gate_hbm.at[0], gate_w, load_sem.at[0]),
+        pltpu.make_async_copy(up_hbm.at[0], up_w, load_sem.at[1]),
+        pltpu.make_async_copy(down_hbm.at[0], down_w, load_sem.at[2]),
+    ]
+    for load in loads:
+        load.start()
+
+    barrier = pltpu.get_barrier_semaphore()
+    for d in range(1, owners):
+        pl.semaphore_signal(barrier, inc=1, device_id={"exp": expert_at(d)}, device_id_type=pl.DeviceIdType.MESH)
+    for q in range(1, splits):
+        pl.semaphore_signal(barrier, inc=1, device_id={"ctx": peer_at(q)}, device_id_type=pl.DeviceIdType.MESH)
+    pl.semaphore_signal(barrier, inc=1, device_id={"rep": 1 - r}, device_id_type=pl.DeviceIdType.MESH)
+
+    routes = routes_ref[...]
+    event_w = weights_ref[...]
+    lane = lax.broadcasted_iota(jnp.int32, (rows, 128), 1)
+    eye = (lax.broadcasted_iota(jnp.int32, (rows, rows), 0) == lax.broadcasted_iota(jnp.int32, (rows, rows), 1)).astype(bf)
+    upper = (lax.broadcasted_iota(jnp.int32, (rows, rows), 0) < lax.broadcasted_iota(jnp.int32, (rows, rows), 1)).astype(bf)
+    lower = (lax.broadcasted_iota(jnp.int32, (rows, rows), 0) > lax.broadcasted_iota(jnp.int32, (rows, rows), 1)).astype(bf)
+    named = ((lane == routes[:, 0:1]) | (lane == routes[:, 1:2])).astype(f32)
+    named_t = lax.dot_general(named.astype(bf), eye, (((0,), (0,)), ((), ())), preferred_element_type=f32)
+    rt_recv[0] = named_t[0:16].astype(bf)
+    places = jnp.dot(lower, named.astype(bf), preferred_element_type=f32)
+
+    def picks(named_rows, expert):
+        row = lax.broadcasted_iota(jnp.int32, (16, rows), 0)
+        pos = jnp.dot(named_rows.astype(bf), upper, preferred_element_type=f32)
+        mine = row == expert
+        pos_e = jnp.sum(jnp.where(mine, pos, 0.0), axis=0, keepdims=True)
+        has_e = jnp.sum(jnp.where(mine, named_rows.astype(f32), 0.0), axis=0, keepdims=True)
+        slot = lax.broadcasted_iota(jnp.int32, (capacity, rows), 0).astype(f32)
+        return ((slot == pos_e) & (has_e > 0.5)).astype(bf)
+
+    pl.semaphore_wait(barrier, owners + splits - 1)
+
+    x_copies, rt_copies = [], []
+    for d in list(range(1, owners)) + [0]:
+        block = jnp.dot(picks(rt_recv[0], expert_at(d)), tokens_ref[...], preferred_element_type=f32).astype(bf)
+        if d == 0:
+            x_recv[0] = block
+            continue
+        x_send[d] = block
+        rt = remote(rt_recv.at[0], rt_recv.at[d], rt_ssem.at[d], rt_rsem.at[d], exp=expert_at(d))
+        cp = remote(x_send.at[d], x_recv.at[d], x_ssem.at[d], x_rsem.at[d], exp=expert_at(d))
+        rt.start()
+        cp.start()
+        rt_copies.append(rt)
+        x_copies.append(cp)
+
+    my_half = pl.ds(pl.multiple_of(r * half, half), half)
+
+    def far(src, j, going_up):
+        sem = far_up if going_up else far_down
+        return remote(src, cots.at[j, my_half], sem.at[j], far_rsem.at[j], exp=z + (1 if going_up else -1))
+
+    def sibling(j):
+        return remote(cots.at[j, my_half], cots.at[j, my_half], sib_ssem.at[j], sib_rsem.at[j], rep=1 - r)
+
+    @pl.when(z < owners - 1)
+    def _():
+        far(cot_ref.at[my_half], z, True).start()
+
+    @pl.when(z > 0)
+    def _():
+        far(cot_ref.at[my_half], z, False).start()
+
+    cots[z] = cot_ref[...]
+
+    def pass_on(d):
+        @pl.when(z - d >= 0)
+        def _():
+            j = z - d
+            far(cots.at[j, my_half], j, True).wait_recv()
+
+            @pl.when(z < owners - 1)
+            def _():
+                far(cots.at[j, my_half], j, True).start()
+
+            sibling(j).start()
+
+        @pl.when(z + d < owners)
+        def _():
+            j = z + d
+            far(cots.at[j, my_half], j, False).wait_recv()
+
+            @pl.when(z > 0)
+            def _():
+                far(cots.at[j, my_half], j, False).start()
+
+            sibling(j).start()
+
+    for load in loads:
+        load.wait()
+
+    def slices(p):
+        return slice(p * part_f, (p + 1) * part_f)
+
+    def first(d):
+        x = x_recv[d]
+        for p in range(splits):
+            part[d, p, 0:capacity] = jnp.dot(x, gate_w[:, slices(p)], preferred_element_type=f32).astype(bf)
+            part[d, p, capacity:2 * capacity] = jnp.dot(x, up_w[:, slices(p)], preferred_element_type=f32).astype(bf)
+
+    def back(d):
+        rows_in = jnp.dot(picks(rt_recv[d], z), cots[source_at(d)], preferred_element_type=f32).astype(bf)
+        for p in range(splits):
+            part[d, p, 2 * capacity:3 * capacity] = lax.dot_general(
+                rows_in, down_w[slices(p), :], (((1,), (1,)), ((), ())), preferred_element_type=f32
+            ).astype(bf)
+
+    def rs(d, q):
+        at = pl.ds(0, 2 * capacity)
+        return remote(part.at[d, peer_at(q), at], shares.at[d, q, at], rs_ssem.at[d, q], rs_rsem.at[d, q], ctx=peer_at(q))
+
+    def bk(d, q):
+        at = pl.ds(2 * capacity, capacity)
+        return remote(part.at[d, peer_at(q), at], shares.at[d, q, at], bk_ssem.at[d, q], bk_rsem.at[d, q], ctx=peer_at(q))
+
+    def ag(d, q):
+        return remote(acts.at[d, c], acts.at[d, c], ag_ssem.at[d, q], ag_rsem.at[d, q], ctx=peer_at(q))
+
+    def gg(d, q):
+        return remote(grads.at[d, c], grads.at[d, c], gg_ssem.at[d, q], gg_rsem.at[d, q], ctx=peer_at(q))
+
+    def out(d):
+        return remote(out_send.at[d], out_recv.at[d], out_ssem.at[d], out_rsem.at[d], exp=source_at(d))
+
+    def eg(d):
+        return remote(eg_send.at[d], eg_recv.at[d], eg_ssem.at[d], eg_rsem.at[d], exp=source_at(d))
+
+    others = range(1, splits)
+
+    for d in range(owners):
+        if d > 0:
+            x_copies[d - 1].wait_recv()
+            rt_copies[d - 1].wait_recv()
+        first(d)
+        for q in others:
+            rs(d, q).start()
+        if d > 0:
+            pass_on(d)
+
+    def activate_block(d):
+        for q in others:
+            rs(d, q).wait_recv()
+        both = part[d, c, 0:2 * capacity].astype(f32)
+        for q in others:
+            both = both + shares[d, q, 0:2 * capacity].astype(f32)
+        saved[d] = both
+        gate_pre, up_pre = both[0:capacity], both[capacity:]
+        acts[d, c] = (gate_pre * jax.nn.sigmoid(gate_pre) * up_pre).astype(bf)
+        for q in others:
+            ag(d, q).start()
+
+    def back_block(d):
+        if d > 0:
+            @pl.when(z >= d)
+            def _():
+                sibling(z - d).wait_recv()
+
+            @pl.when(z < d)
+            def _():
+                sibling(z - d + owners).wait_recv()
+        back(d)
+        for q in others:
+            bk(d, q).start()
+
+    for d in range(owners):
+        activate_block(d)
+        back_block(d)
+
+    def out_block(d):
+        for q in others:
+            ag(d, q).wait_recv()
+        target = out_recv if d == 0 else out_send
+        act = jnp.concatenate([acts[d, p] for p in range(splits)], axis=1)
+        target[d] = jnp.dot(act, down_w[...], preferred_element_type=f32).astype(bf)
+        if d > 0:
+            out(d).start()
+
+    def grad_block(d):
+        for q in others:
+            bk(d, q).wait_recv()
+        back_pre = part[d, c, 2 * capacity:].astype(f32)
+        for q in others:
+            back_pre = back_pre + shares[d, q, 2 * capacity:].astype(f32)
+        gate_pre, up_pre = saved[d, 0:capacity], saved[d, capacity:]
+        squash = jax.nn.sigmoid(gate_pre)
+        grads[d, c, 0:capacity] = (back_pre * up_pre * squash * (1.0 + gate_pre * (1.0 - squash))).astype(bf)
+        grads[d, c, capacity:] = (back_pre * gate_pre * squash).astype(bf)
+        for q in others:
+            gg(d, q).start()
+
+    order = list(range(1, owners)) + [0]
+    for d in order:
+        out_block(d)
+        grad_block(d)
+
+    def eg_block(d):
+        for q in others:
+            gg(d, q).wait_recv()
+        target = eg_recv if d == 0 else eg_send
+        gate_g = jnp.concatenate([grads[d, p, 0:capacity] for p in range(splits)], axis=1)
+        up_g = jnp.concatenate([grads[d, p, capacity:] for p in range(splits)], axis=1)
+        step = 256 if columns % 256 == 0 else columns
+        for n in range(0, columns, step):
+            nt = (((1,), (1,)), ((), ()))
+            target[d, :, n:n + step] = (
+                lax.dot_general(gate_g, gate_w[n:n + step], nt, preferred_element_type=f32)
+                + lax.dot_general(up_g, up_w[n:n + step], nt, preferred_element_type=f32)
+            ).astype(bf)
+        if d > 0:
+            eg(d).start()
+
+    for d in order:
+        eg_block(d)
+
+    def chosen(d):
+        expert = expert_at(d)
+        mine = lane == expert
+        pos = jnp.sum(jnp.where(mine, places, 0.0), axis=1, keepdims=True)
+        has = jnp.sum(jnp.where(mine, named, 0.0), axis=1, keepdims=True)
+        weight = jnp.sum(jnp.where(routes == expert, event_w, 0.0), axis=1, keepdims=True)
+        slot = lax.broadcasted_iota(jnp.int32, (rows, capacity), 1).astype(f32)
+        return ((slot == pos) & (has > 0.5)).astype(bf), weight, expert
+
+    step = 256 if columns % 256 == 0 else columns
+
+    def collect(d, recv, into, last, with_dot):
+        pick, weight, expert = chosen(d)
+        dots = jnp.zeros((rows, 1), f32)
+        for n in range(0, columns, step):
+            at = slice(n, n + step)
+            row = jnp.dot(pick, recv[d, :, at], preferred_element_type=f32)
+            total = weight * row
+            if d > 0:
+                total = total + mix_acc[:, at]
+            if last:
+                into[:, at] = total.astype(bf)
+            else:
+                mix_acc[:, at] = total
+            if with_dot:
+                dots = dots + jnp.sum(row * cot_ref[:, at].astype(f32), axis=1, keepdims=True)
+        return dots, expert
+
+    acc = jnp.zeros((rows, 128), f32)
+    wide = jnp.where(lane == 0, routes[:, 0:1], jnp.where(lane == 1, routes[:, 1:2], -1))
+    for d in range(owners):
+        if d > 0:
+            out(d).wait_recv()
+        dots, expert = collect(d, out_recv, mixed_ref, d == owners - 1, True)
+        acc = acc + jnp.where(wide == expert, dots, 0.0)
+    wg_parts[0] = acc
+
+    def wg(q):
+        return remote(wg_parts.at[0], wg_parts.at[q], wg_ssem.at[q], wg_rsem.at[q], ctx=peer_at(q))
+
+    for q in others:
+        wg(q).start()
+    for d in range(owners):
+        if d > 0:
+            eg(d).wait_recv()
+        collect(d, eg_recv, grad_ref, d == owners - 1, False)
+    for q in others:
+        wg(q).wait_recv()
+        acc = acc + wg_parts[q]
+    wgrad_ref[...] = acc[:, 0:2]
+
+    for d in range(1, owners):
+        x_copies[d - 1].wait_send()
+        rt_copies[d - 1].wait_send()
+        out(d).wait_send()
+        eg(d).wait_send()
+    for q in others:
+        wg(q).wait_send()
+        for d in range(owners):
+            rs(d, q).wait_send()
+            bk(d, q).wait_send()
+            ag(d, q).wait_send()
+            gg(d, q).wait_send()
+
+    @pl.when(z < owners - 1)
+    def _():
+        far(cot_ref.at[my_half], z, True).wait_send()
+
+    @pl.when(z > 0)
+    def _():
+        far(cot_ref.at[my_half], z, False).wait_send()
+
+    for d in range(1, owners):
+        @pl.when(z - d >= 0)
+        def _():
+            @pl.when(z < owners - 1)
+            def _():
+                far(cots.at[z - d, my_half], z - d, True).wait_send()
+
+            sibling(z - d).wait_send()
+
+        @pl.when(z + d < owners)
+        def _():
+            @pl.when(z > 0)
+            def _():
+                far(cots.at[z + d, my_half], z + d, False).wait_send()
+
+            sibling(z + d).wait_send()
+
+
+def shards_fused(tokens, routes, event_weights, cotangent, w_gate, w_up, w_down):
+    owners, splits = lax.axis_size("exp"), lax.axis_size("ctx")
+    _, columns, hidden = w_gate.shape
+    rows, fanout = routes.shape
+    capacity = max(2, 5 * rows * fanout // (4 * owners))
+    part_f = hidden // splits
+    sizes = (owners, splits, capacity, rows, columns, hidden)
+    bf, f32 = jnp.bfloat16, jnp.float32
+    vmem, dma = pltpu.VMEM, pltpu.SemaphoreType.DMA
+    full = pl.BlockSpec(memory_space=pltpu.VMEM)
+    anywhere = pl.BlockSpec(memory_space=pl.ANY)
+    per_block = dma((owners,))
+    per_pair = dma((owners, splits))
+    moved = owners * capacity * columns
+    return pl.pallas_call(
+        functools.partial(fused, sizes),
+        out_shape=(
+            jax.ShapeDtypeStruct((rows, columns), bf),
+            jax.ShapeDtypeStruct((rows, columns), bf),
+            jax.ShapeDtypeStruct((rows, fanout), f32),
+        ),
+        in_specs=[full, full, full, full, anywhere, anywhere, anywhere],
+        out_specs=(full, full, full),
+        scratch_shapes=[
+            vmem((columns, hidden), bf), vmem((columns, hidden), bf), vmem((hidden, columns), bf),
+            vmem((owners, capacity, columns), bf), vmem((owners, capacity, columns), bf),
+            vmem((owners, 16, rows), bf),
+            vmem((owners, rows, columns), bf),
+            vmem((owners, splits, 3 * capacity, part_f), bf),
+            vmem((owners, splits, 3 * capacity, part_f), bf),
+            vmem((owners, splits, capacity, part_f), bf),
+            vmem((owners, splits, 2 * capacity, part_f), bf),
+            vmem((owners, 2 * capacity, part_f), f32),
+            vmem((owners, capacity, columns), bf), vmem((owners, capacity, columns), bf),
+            vmem((owners, capacity, columns), bf), vmem((owners, capacity, columns), bf),
+            vmem((splits, rows, 128), f32),
+            vmem((rows, columns), f32),
+            dma((3,)), per_block, per_block, per_block, per_block,
+            per_block, per_block, per_block, per_block, per_block,
+            per_pair, per_pair, per_pair, per_pair, per_pair, per_pair, per_pair, per_pair,
+            per_block, per_block, per_block, per_block, dma((splits,)), dma((splits,)),
+        ],
+        compiler_params=pltpu.CompilerParams(
+            collective_id=0, has_side_effects=True, vmem_limit_bytes=56 * 1024 * 1024
+        ),
+        cost_estimate=pl.CostEstimate(
+            flops=12 * moved * hidden, bytes_accessed=6 * columns * hidden, transcendentals=0
+        ),
+    )(routes, event_weights, tokens, cotangent, w_gate, w_up, w_down)
+
+
+def fits(mesh, w_gate, routes):
+    owners, splits, cores = mesh.shape["exp"], mesh.shape["ctx"], mesh.shape["rep"]
+    experts, depth, hidden = w_gate.shape
+    rows, fanout = routes.shape[0] // (owners * cores), routes.shape[1]
+    capacity = max(2, 5 * rows * fanout // (4 * experts))
+    columns = depth // splits
+    return (
+        experts == owners and 1 < owners <= 8 and splits > 1 and cores == 2 and fanout == 2
+        and rows == 128 and capacity % 16 == 0 and columns % 128 == 0 and hidden % (128 * splits) == 0
+        and 6 * columns * hidden <= 16 * 1024 * 1024
+    )
+
+
 def solution(mesh):
     in_specs = (
         P(("rep", "exp"), "ctx"),
@@ -115,4 +526,10 @@
         P("exp", None, "ctx"),
     )
     out_specs = (P(("rep", "exp"), "ctx"), P(("rep", "exp"), "ctx"), P(("rep", "exp"), None))
-    return jax.shard_map(shards, mesh=mesh, in_specs=in_specs, out_specs=out_specs, check_vma=False)
+
+    def run(tokens, routes, event_weights, cotangent, w_gate, w_up, w_down):
+        body = shards_fused if fits(mesh, w_gate, routes) else shards
+        mapped = jax.shard_map(body, mesh=mesh, in_specs=in_specs, out_specs=out_specs, check_vma=False)
+        return mapped(tokens, routes, event_weights, cotangent, w_gate, w_up, w_down)
+
+    return run

time: 236 us -> 117 us (0.50)
  Pallas kernels: 0 us -> 108 us
  waiting for transfers between devices: 103 us -> 0 us
  blocking collectives: 50.6 us -> 0 us
  matrix products: 19.6 us -> 0 us
  starting transfers between devices: 18 us -> 0 us
  other arithmetic: 15 us -> 0 us
  between operations: 14.2 us -> 0.64 us
  local copies, waits for them, and re-layouts: 14.5 us -> 7.93 us
    pallas_call x0 -> x1, Pallas kernels: none -> 108 us  [shards_fused(): pl.pallas_call(functools.partial(fused, sizes), out_shape=(jax.ShapeDtype...]
    all_to_all x4 -> x0, waiting for transfers between devices: 69.7 us -> none  [the longest x1 21.4 us: shards(): lax.all_to_all(send_cots, 'exp', split_axis=0, concat_axis=0, tiled=True)]
    all_gather x3 -> x0, blocking collectives: 41.1 us -> none  [the longest x1 15.7 us: shards(): lax.all_gather(up_share, 'ctx', axis=0, tiled=True)]
    reduce_scatter x1 -> x0, waiting for transfers between devices: 33.4 us -> none  [shards(): lax.psum_scatter(jnp.stack([jnp.einsum('jsd,jdf->fjs', expert_in, w_gate,...]
    dot_general x7 -> x0, matrix products: 19.6 us -> none  [the longest x1 4.39 us: shards(): jnp.einsum('fjs,jfd->jsd', hidden_act, w_down, preferred_element_type=jnp...]
    all_to_all x4 -> x0, starting transfers between devices: 17.9 us -> none  [the longest x1 6.32 us: shards(): lax.all_to_all(send_tokens, 'exp', split_axis=0, concat_axis=0, tiled=True)]
    psum x1 -> x0, blocking collectives: 9.48 us -> none  [shards(): weight_grad = lax.psum(weight_part, 'ctx')]
    reduce_sum x3 -> x0, other arithmetic: 6.97 us -> none  [the longest x1 3.59 us: shards(): jnp.sum(event_weights[:, :, None] * out_rows, axis=1).astype(jnp.bfloat16)]
  transfers between devices with their start and end apart: 5 -> 0, of which waited for: 5 -> 0; matrix products, arithmetic and copies ran while one was open for 10% -> 0% of each run, Pallas kernels for 0% -> 0%
where the time goes in v1:
time: 117 us
  Pallas kernels  108 us (92%)
  local copies, waits for them, and re-layouts  7.93 us (7%)
    pallas_call x1, Pallas kernels, shards_fused(): pl.pallas_call(functools.partial(fused, sizes), out_shape=(jax.ShapeDtype...  108 us
    unnamed x4, local copies, waits for them, and re-layouts  6.46 us

profile of v1, /device:TPU:0, one launch (start us, length us, event | category | flops | bytes accessed | tf_op | source)
XLA Modules:
  0.0 116.9 jit_solution(13477836850234196312)
XLA Ops:
  0.6 1.4 %copy.10.routes_ref = s32[128,2]{1,0:T(8,128)} copy(s32[128,2]{0,1:T(2,128)} %param.8) | data formatting | bytes 2048 | tf_op args[1]
  2.0 1.4 %copy.11.weights_ref = f32[128,2]{1,0:T(8,128)} copy(f32[128,2]{0,1:T(2,128)} %param.9) | data formatting | bytes 2048 | tf_op args[2]
  3.5 108.3 %shard_map.94 = (bf16[128,1792]{1,0:T(8,128)(2,1)}, bf16[128,1792]{1,0:T(8,128)(2,1)}, f32[128,2]{1,0:T(8,128)}) custom-call(s32[128,2]{1,0:T(8,128)} %copy.10.routes_ref, f32[128,2]{1,0:T(8,128)} %copy.11.weights_ref, bf16[128,1792]{1,0:T(8,128)(2,1)} %tokens_ref.1, bf16[128,1792]{1,0:T(8,128)(2,1)} %cot_ref.1, bf16[1,1792,1024]{2,1,0:T(8,128)(2,1)} %gate_hbm.1, ...), custom_call_target="tpu_custom_call" | custom-call | flops 7046430720 | bytes 11010048 | tf_op jit(solution)/shard_map/pallas_call | solution.py:468
  111.8 1.5 %copy.12 = f32[128,2]{0,1:T(2,128)} copy(f32[128,2]{1,0:T(8,128)} %get-tuple-element.5) | data formatting | bytes 2048 | tf_op jit(solution)/shard_map/pallas_call | solution.py:468
  113.3 1.8 %copy.15 = bf16[128,1792]{1,0:T(8,128)(2,1)} copy(bf16[128,1792]{1,0:T(8,128)(2,1)} %get-tuple-element.9) | data formatting | bytes 917504
  115.1 1.8 %copy.16 = bf16[128,1792]{1,0:T(8,128)(2,1)} copy(bf16[128,1792]{1,0:T(8,128)(2,1)} %get-tuple-element.10) | data formatting | bytes 917504

commit v2 on v1

--- a/solution.py
+++ b/solution.py
@@ -159,19 +159,26 @@
 
     routes = routes_ref[...]
     event_w = weights_ref[...]
-    lane = lax.broadcasted_iota(jnp.int32, (rows, 128), 1)
-    eye = (lax.broadcasted_iota(jnp.int32, (rows, rows), 0) == lax.broadcasted_iota(jnp.int32, (rows, rows), 1)).astype(bf)
-    upper = (lax.broadcasted_iota(jnp.int32, (rows, rows), 0) < lax.broadcasted_iota(jnp.int32, (rows, rows), 1)).astype(bf)
-    lower = (lax.broadcasted_iota(jnp.int32, (rows, rows), 0) > lax.broadcasted_iota(jnp.int32, (rows, rows), 1)).astype(bf)
-    named = ((lane == routes[:, 0:1]) | (lane == routes[:, 1:2])).astype(f32)
-    named_t = lax.dot_general(named.astype(bf), eye, (((0,), (0,)), ((), ())), preferred_element_type=f32)
-    rt_recv[0] = named_t[0:16].astype(bf)
+    row_i = lax.broadcasted_iota(jnp.int32, (rows, rows), 0)
+    col_i = lax.broadcasted_iota(jnp.int32, (rows, rows), 1)
+    eye, upper, lower = row_i == col_i, (row_i < col_i).astype(bf), (row_i > col_i).astype(bf)
+    experts_i = lax.broadcasted_iota(jnp.int32, (16, rows), 0)
+    named_t = ((experts_i == routes[0:1]) | (experts_i == routes[1:2])).astype(f32).astype(bf)
+    rt_recv[0] = named_t
+    named = lax.dot_general(eye.astype(f32).astype(bf), named_t, (((1,), (1,)), ((), ())), preferred_element_type=f32)
     places = jnp.dot(lower, named.astype(bf), preferred_element_type=f32)
 
+    def line(i):
+        near = jnp.minimum(z, owners - 1 - z)
+        paired = i <= 2 * near
+        distance = jnp.where(paired, (i + 1) // 2, i - near)
+        ahead = jnp.where(paired, i % 2 == 0, z < owners - 1 - z)
+        other = z + jnp.where(ahead, distance, -distance)
+        return other, lax.rem(z - other + owners, owners), lax.rem(other - z + owners, owners)
+
     def picks(named_rows, expert):
-        row = lax.broadcasted_iota(jnp.int32, (16, rows), 0)
-        pos = jnp.dot(named_rows.astype(bf), upper, preferred_element_type=f32)
-        mine = row == expert
+        pos = jnp.dot(named_rows, upper, preferred_element_type=f32)
+        mine = experts_i == expert
         pos_e = jnp.sum(jnp.where(mine, pos, 0.0), axis=0, keepdims=True)
         has_e = jnp.sum(jnp.where(mine, named_rows.astype(f32), 0.0), axis=0, keepdims=True)
         slot = lax.broadcasted_iota(jnp.int32, (capacity, rows), 0).astype(f32)
@@ -179,19 +186,27 @@
 
     pl.semaphore_wait(barrier, owners + splits - 1)
 
-    x_copies, rt_copies = [], []
-    for d in list(range(1, owners)) + [0]:
-        block = jnp.dot(picks(rt_recv[0], expert_at(d)), tokens_ref[...], preferred_element_type=f32).astype(bf)
-        if d == 0:
-            x_recv[0] = block
-            continue
-        x_send[d] = block
-        rt = remote(rt_recv.at[0], rt_recv.at[d], rt_ssem.at[d], rt_rsem.at[d], exp=expert_at(d))
-        cp = remote(x_send.at[d], x_recv.at[d], x_ssem.at[d], x_rsem.at[d], exp=expert_at(d))
-        rt.start()
-        cp.start()
-        rt_copies.append(rt)
-        x_copies.append(cp)
+    steps = range(1, owners)
+
+    def rt(i):
+        other, _, d = line(i)
+        return remote(rt_recv.at[0], rt_recv.at[d], rt_ssem.at[i], rt_rsem.at[d], exp=other)
+
+    def send_x(i):
+        other, _, d = line(i)
+        return remote(x_send.at[i], x_recv.at[d], x_ssem.at[i], x_rsem.at[d], exp=other)
+
+    def got_x(i):
+        other, d, _ = line(i)
+        remote(rt_recv.at[0], rt_recv.at[d], rt_ssem.at[i], rt_rsem.at[d], exp=other).wait_recv()
+        remote(x_send.at[i], x_recv.at[d], x_ssem.at[i], x_rsem.at[d], exp=other).wait_recv()
+        return d
+
+    for i in steps:
+        rt(i).start()
+    for i in steps:
+        x_send[i] = jnp.dot(picks(rt_recv[0], line(i)[0]), tokens_ref[...], preferred_element_type=f32).astype(bf)
+        send_x(i).start()
 
     my_half = pl.ds(pl.multiple_of(r * half, half), half)
 
@@ -211,6 +226,7 @@
         far(cot_ref.at[my_half], z, False).start()
 
     cots[z] = cot_ref[...]
+    x_recv[0] = jnp.dot(picks(rt_recv[0], z), tokens_ref[...], preferred_element_type=f32).astype(bf)
 
     def pass_on(d):
         @pl.when(z - d >= 0)
@@ -268,23 +284,15 @@
     def gg(d, q):
         return remote(grads.at[d, c], grads.at[d, c], gg_ssem.at[d, q], gg_rsem.at[d, q], ctx=peer_at(q))
 
-    def out(d):
-        return remote(out_send.at[d], out_recv.at[d], out_ssem.at[d], out_rsem.at[d], exp=source_at(d))
-
-    def eg(d):
-        return remote(eg_send.at[d], eg_recv.at[d], eg_ssem.at[d], eg_rsem.at[d], exp=source_at(d))
+    def out(i):
+        other, d, _ = line(i)
+        return remote(out_send.at[i], out_recv.at[d], out_ssem.at[i], out_rsem.at[d], exp=other)
+
+    def eg(i):
+        other, d, _ = line(i)
+        return remote(eg_send.at[i], eg_recv.at[d], eg_ssem.at[i], eg_rsem.at[d], exp=other)
 
     others = range(1, splits)
-
-    for d in range(owners):
-        if d > 0:
-            x_copies[d - 1].wait_recv()
-            rt_copies[d - 1].wait_recv()
-        first(d)
-        for q in others:
-            rs(d, q).start()
-        if d > 0:
-            pass_on(d)
 
     def activate_block(d):
         for q in others:
@@ -298,31 +306,33 @@
         for q in others:
             ag(d, q).start()
 
-    def back_block(d):
-        if d > 0:
-            @pl.when(z >= d)
-            def _():
-                sibling(z - d).wait_recv()
-
-            @pl.when(z < d)
-            def _():
-                sibling(z - d + owners).wait_recv()
+    def back_block(i):
+        d = 0
+        if i > 0:
+            other, d, _ = line(i)
+            sibling(other).wait_recv()
         back(d)
         for q in others:
             bk(d, q).start()
 
-    for d in range(owners):
-        activate_block(d)
-        back_block(d)
-
-    def out_block(d):
+    def first_block(i):
+        d = got_x(i) if i else 0
+        first(d)
+        for q in others:
+            rs(d, q).start()
+
+    def slot(i):
+        return line(i)[1] if i else 0
+
+    def out_block(i):
+        d = slot(i)
         for q in others:
             ag(d, q).wait_recv()
-        target = out_recv if d == 0 else out_send
         act = jnp.concatenate([acts[d, p] for p in range(splits)], axis=1)
-        target[d] = jnp.dot(act, down_w[...], preferred_element_type=f32).astype(bf)
-        if d > 0:
-            out(d).start()
+        target = out_send if i else out_recv
+        target[i] = jnp.dot(act, down_w[...], preferred_element_type=f32).astype(bf)
+        if i:
+            out(i).start()
 
     def grad_block(d):
         for q in others:
@@ -337,86 +347,107 @@
         for q in others:
             gg(d, q).start()
 
-    order = list(range(1, owners)) + [0]
-    for d in order:
-        out_block(d)
-        grad_block(d)
-
-    def eg_block(d):
+    def eg_block(i):
+        d = slot(i)
         for q in others:
             gg(d, q).wait_recv()
-        target = eg_recv if d == 0 else eg_send
+        target = eg_send if i else eg_recv
         gate_g = jnp.concatenate([grads[d, p, 0:capacity] for p in range(splits)], axis=1)
         up_g = jnp.concatenate([grads[d, p, capacity:] for p in range(splits)], axis=1)
         step = 256 if columns % 256 == 0 else columns
         for n in range(0, columns, step):
             nt = (((1,), (1,)), ((), ()))
-            target[d, :, n:n + step] = (
+            target[i, :, n:n + step] = (
                 lax.dot_general(gate_g, gate_w[n:n + step], nt, preferred_element_type=f32)
                 + lax.dot_general(up_g, up_w[n:n + step], nt, preferred_element_type=f32)
             ).astype(bf)
-        if d > 0:
-            eg(d).start()
-
-    for d in order:
-        eg_block(d)
-
-    def chosen(d):
-        expert = expert_at(d)
-        mine = lane == expert
+        if i:
+            eg(i).start()
+
+    first_block(0)
+    back_block(0)
+    last = owners - 1
+    for i in steps:
+        first_block(i)
+        activate_block(slot(i - 1))
+        if i > 1:
+            out_block(i - 1)
+        pass_on(i)
+    activate_block(slot(last))
+    for i in steps:
+        back_block(i)
+        if i == 1:
+            out_block(last)
+    grad_block(0)
+    for i in steps:
+        grad_block(slot(i))
+        if i > 1:
+            eg_block(i - 1)
+    eg_block(last)
+    out_block(0)
+    eg_block(0)
+
+    def weight_row(expert):
+        return jnp.sum(jnp.where(routes == expert, event_w, 0.0), axis=0, keepdims=True)
+
+    def chosen(expert):
+        mine = lax.broadcasted_iota(jnp.int32, (rows, 16), 1) == expert
         pos = jnp.sum(jnp.where(mine, places, 0.0), axis=1, keepdims=True)
         has = jnp.sum(jnp.where(mine, named, 0.0), axis=1, keepdims=True)
-        weight = jnp.sum(jnp.where(routes == expert, event_w, 0.0), axis=1, keepdims=True)
-        slot = lax.broadcasted_iota(jnp.int32, (rows, capacity), 1).astype(f32)
-        return ((slot == pos) & (has > 0.5)).astype(bf), weight, expert
+        weight = jnp.sum(jnp.where(eye, weight_row(expert), 0.0), axis=1, keepdims=True)
+        place = lax.broadcasted_iota(jnp.int32, (rows, capacity), 1).astype(f32)
+        return ((place == pos) & (has > 0.5)).astype(bf), weight
 
     step = 256 if columns % 256 == 0 else columns
 
-    def collect(d, recv, into, last, with_dot):
-        pick, weight, expert = chosen(d)
+    def collect(i, recv, into, with_dot):
+        expert, d = z, 0
+        if i:
+            expert, _, d = line(i)
+        pick, weight = chosen(expert)
         dots = jnp.zeros((rows, 1), f32)
         for n in range(0, columns, step):
             at = slice(n, n + step)
             row = jnp.dot(pick, recv[d, :, at], preferred_element_type=f32)
             total = weight * row
-            if d > 0:
+            if i > 0:
                 total = total + mix_acc[:, at]
-            if last:
+            if i == last:
                 into[:, at] = total.astype(bf)
             else:
                 mix_acc[:, at] = total
             if with_dot:
                 dots = dots + jnp.sum(row * cot_ref[:, at].astype(f32), axis=1, keepdims=True)
-        return dots, expert
-
-    acc = jnp.zeros((rows, 128), f32)
-    wide = jnp.where(lane == 0, routes[:, 0:1], jnp.where(lane == 1, routes[:, 1:2], -1))
-    for d in range(owners):
-        if d > 0:
-            out(d).wait_recv()
-        dots, expert = collect(d, out_recv, mixed_ref, d == owners - 1, True)
-        acc = acc + jnp.where(wide == expert, dots, 0.0)
-    wg_parts[0] = acc
+        if not with_dot:
+            return None
+        return jnp.where(routes == expert, jnp.sum(jnp.where(eye, dots, 0.0), axis=0, keepdims=True), 0.0)
 
     def wg(q):
         return remote(wg_parts.at[0], wg_parts.at[q], wg_ssem.at[q], wg_rsem.at[q], ctx=peer_at(q))
 
+    acc = jnp.zeros(routes.shape, f32)
+    for i in range(owners):
+        if i:
+            remote(out_send.at[i], out_recv.at[line(i)[2]], out_ssem.at[i], out_rsem.at[line(i)[2]], exp=line(i)[0]).wait_recv()
+        acc = acc + collect(i, out_recv, mixed_ref, True)
+    wg_parts[0, 0:routes.shape[0]] = acc
+    wg_parts[0, routes.shape[0]:] = jnp.zeros((8 - routes.shape[0], rows), f32)
     for q in others:
         wg(q).start()
-    for d in range(owners):
-        if d > 0:
-            eg(d).wait_recv()
-        collect(d, eg_recv, grad_ref, d == owners - 1, False)
+    for i in range(owners):
+        if i:
+            remote(eg_send.at[i], eg_recv.at[line(i)[2]], eg_ssem.at[i], eg_rsem.at[line(i)[2]], exp=line(i)[0]).wait_recv()
+        collect(i, eg_recv, grad_ref, False)
     for q in others:
         wg(q).wait_recv()
-        acc = acc + wg_parts[q]
-    wgrad_ref[...] = acc[:, 0:2]
-
-    for d in range(1, owners):
-        x_copies[d - 1].wait_send()
-        rt_copies[d - 1].wait_send()
-        out(d).wait_send()
-        eg(d).wait_send()
+        acc = acc + wg_parts[q, 0:routes.shape[0]]
+    wgrad_ref[...] = acc
+
+    for i in steps:
+        send_x(i).wait_send()
+        rt(i).wait_send()
+        out(i).wait_send()
+        eg(i).wait_send()
     for q in others:
         wg(q).wait_send()
         for d in range(owners):
@@ -449,6 +480,11 @@
                 far(cots.at[z + d, my_half], z + d, False).wait_send()
 
             sibling(z + d).wait_send()
+
+
+def hand_over(*refs):
+    for source, target in zip(refs[:3], refs[3:]):
+        target[...] = source[...]
 
 
 def shards_fused(tokens, routes, event_weights, cotangent, w_gate, w_up, w_down):
@@ -465,12 +501,12 @@
     per_block = dma((owners,))
     per_pair = dma((owners, splits))
     moved = owners * capacity * columns
-    return pl.pallas_call(
+    results = pl.pallas_call(
         functools.partial(fused, sizes),
         out_shape=(
             jax.ShapeDtypeStruct((rows, columns), bf),
             jax.ShapeDtypeStruct((rows, columns), bf),
-            jax.ShapeDtypeStruct((rows, fanout), f32),
+            jax.ShapeDtypeStruct((fanout, rows), f32),
         ),
         in_specs=[full, full, full, full, anywhere, anywhere, anywhere],
         out_specs=(full, full, full),
@@ -486,7 +522,7 @@
             vmem((owners, 2 * capacity, part_f), f32),
             vmem((owners, capacity, columns), bf), vmem((owners, capacity, columns), bf),
             vmem((owners, capacity, columns), bf), vmem((owners, capacity, columns), bf),
-            vmem((splits, rows, 128), f32),
+            vmem((splits, 8, rows), f32),
             vmem((rows, columns), f32),
             dma((3,)), per_block, per_block, per_block, per_block,
             per_block, per_block, per_block, per_block, per_block,
@@ -499,7 +535,15 @@
         cost_estimate=pl.CostEstimate(
             flops=12 * moved * hidden, bytes_accessed=6 * columns * hidden, transcendentals=0
         ),
-    )(routes, event_weights, tokens, cotangent, w_gate, w_up, w_down)
+    )(routes.T, event_weights.T, tokens, cotangent, w_gate, w_up, w_down)
+    mixed, token_grad, weight_grad = pl.pallas_call(
+        hand_over,
+        out_shape=tuple(jax.ShapeDtypeStruct(x.shape, x.dtype) for x in results),
+        in_specs=[full] * 3,
+        out_specs=(full,) * 3,
+        cost_estimate=pl.CostEstimate(flops=0, bytes_accessed=8 * rows * columns, transcendentals=0),
+    )(*results)
+    return mixed, token_grad, weight_grad.T
 
 
 def fits(mesh, w_gate, routes):

time: 117 us -> 105 us (0.90); the launches traced: 117 us -> 104 us
  local copies, waits for them, and re-layouts: 7.93 us -> 0 us
  Pallas kernels: 108 us -> 103 us
    pallas_call x1, Pallas kernels: 108 us -> 101 us  [shards_fused(): pl.pallas_call(functools.partial(fused, sizes), out_shape=(jax.ShapeDtype...]
    unnamed x4 -> x0, local copies, waits for them, and re-layouts: 6.46 us -> none
    pallas_call x0 -> x1, Pallas kernels: none -> 2.11 us  [shards_fused(): pl.pallas_call(hand_over, out_shape=tuple((jax.ShapeDtypeStruct(x.shape,...]
    pallas_call x1 -> x0, local copies, waits for them, and re-layouts: 1.48 us -> none  [shards_fused(): pl.pallas_call(functools.partial(fused, sizes), out_shape=(jax.ShapeDtype...]
where the time goes in v2:
time: 105 us; the launch traced here: 104 us
  Pallas kernels  103 us (98%)
    pallas_call x1, Pallas kernels, shards_fused(): pl.pallas_call(functools.partial(fused, sizes), out_shape=(jax.ShapeDtype...  101 us
    pallas_call x1, Pallas kernels, shards_fused(): pl.pallas_call(hand_over, out_shape=tuple((jax.ShapeDtypeStruct(x.shape,...  2.11 us

profile of v2, /device:TPU:0, one launch (start us, length us, event | category | flops | bytes accessed | tf_op | source)
XLA Modules:
  0.0 103.5 jit_solution(13013070194890282704)
XLA Ops:
  0.6 100.8 %shard_map.94 = (bf16[128,1792]{1,0:T(8,128)(2,1)}, bf16[128,1792]{1,0:T(8,128)(2,1)}, f32[2,128]{1,0:T(2,128)}) custom-call(s32[2,128]{1,0:T(2,128)} %bitcast.3, f32[2,128]{1,0:T(2,128)} %bitcast.4, bf16[128,1792]{1,0:T(8,128)(2,1)} %tokens_ref.1, bf16[128,1792]{1,0:T(8,128)(2,1)} %cot_ref.1, bf16[1,1792,1024]{2,1,0:T(8,128)(2,1)} %gate_hbm.1, ...), custom_call_target="tpu_custom_call" | custom-call | flops 7046430720 | bytes 11010048 | tf_op jit(solution)/shard_map/pallas_call | solution.py:504
  101.4 2.1 %shard_map.95 = (bf16[128,1792]{1,0:T(8,128)(2,1)}, bf16[128,1792]{1,0:T(8,128)(2,1)}, f32[2,128]{1,0:T(2,128)}) custom-call(bf16[128,1792]{1,0:T(8,128)(2,1)} %get-tuple-element.9.refs_0_, bf16[128,1792]{1,0:T(8,128)(2,1)} %get-tuple-element.10.refs_1_, f32[2,128]{1,0:T(2,128)} %get-tuple-element.11.refs_2_), custom_call_target="tpu_custom_call" | custom-call | bytes 1835008 | tf_op jit(solution)/shard_map/pallas_call | solution.py:539

commit v3 on v2

--- a/solution.py
+++ b/solution.py
@@ -113,10 +113,10 @@
     routes_ref, weights_ref, tokens_ref, cot_ref, gate_hbm, up_hbm, down_hbm,
     mixed_ref, grad_ref, wgrad_ref,
     gate_w, up_w, down_w, x_send, x_recv, rt_recv, cots, part, shares, acts, grads, saved,
-    out_send, out_recv, eg_send, eg_recv, wg_parts, mix_acc,
+    stack, sums, sum_recv, pair_picks, slot_w, wg_send, wg_recv, wg_parts,
     load_sem, x_ssem, x_rsem, rt_ssem, rt_rsem, far_up, far_down, far_rsem, sib_ssem, sib_rsem,
     rs_ssem, rs_rsem, bk_ssem, bk_rsem, ag_ssem, ag_rsem, gg_ssem, gg_rsem,
-    out_ssem, out_rsem, eg_ssem, eg_rsem, wg_ssem, wg_rsem,
+    pair_ssem, pair_rsem, sum_ssem, sum_rsem, wgz_ssem, wgz_rsem, wg_ssem, wg_rsem,
 ):
     owners, splits, capacity, rows, columns, hidden = sizes
     part_f = hidden // splits
@@ -161,28 +161,33 @@
     event_w = weights_ref[...]
     row_i = lax.broadcasted_iota(jnp.int32, (rows, rows), 0)
     col_i = lax.broadcasted_iota(jnp.int32, (rows, rows), 1)
-    eye, upper, lower = row_i == col_i, (row_i < col_i).astype(bf), (row_i > col_i).astype(bf)
+    upper = (row_i < col_i).astype(f32).astype(bf)
     experts_i = lax.broadcasted_iota(jnp.int32, (16, rows), 0)
-    named_t = ((experts_i == routes[0:1]) | (experts_i == routes[1:2])).astype(f32).astype(bf)
-    rt_recv[0] = named_t
-    named = lax.dot_general(eye.astype(f32).astype(bf), named_t, (((1,), (1,)), ((), ())), preferred_element_type=f32)
-    places = jnp.dot(lower, named.astype(bf), preferred_element_type=f32)
+    rt_recv[0, 0:2] = routes.astype(f32)
+    rt_recv[0, 2:4] = event_w
+    rt_recv[0, 4:] = jnp.zeros((4, rows), f32)
+
+    end = z // 2
+    partner = z + 1 - 2 * lax.rem(z, 2)
+    inner = (z == 1) | (z == 2)
 
     def line(i):
-        near = jnp.minimum(z, owners - 1 - z)
-        paired = i <= 2 * near
-        distance = jnp.where(paired, (i + 1) // 2, i - near)
-        ahead = jnp.where(paired, i % 2 == 0, z < owners - 1 - z)
-        other = z + jnp.where(ahead, distance, -distance)
+        other = (z, partner, 2 - end, 3 * (1 - end))[i]
         return other, lax.rem(z - other + owners, owners), lax.rem(other - z + owners, owners)
 
-    def picks(named_rows, expert):
-        pos = jnp.dot(named_rows, upper, preferred_element_type=f32)
+    def picks(d, expert):
+        r0, r1 = rt_recv[d, 0:1], rt_recv[d, 1:2]
+        experts_f = experts_i.astype(f32)
+        named = ((experts_f == r0) | (experts_f == r1)).astype(f32)
+        pos = jnp.dot(named.astype(bf), upper, preferred_element_type=f32)
         mine = experts_i == expert
         pos_e = jnp.sum(jnp.where(mine, pos, 0.0), axis=0, keepdims=True)
-        has_e = jnp.sum(jnp.where(mine, named_rows.astype(f32), 0.0), axis=0, keepdims=True)
-        slot = lax.broadcasted_iota(jnp.int32, (capacity, rows), 0).astype(f32)
-        return ((slot == pos_e) & (has_e > 0.5)).astype(bf)
+        has_e = jnp.sum(jnp.where(mine, named, 0.0), axis=0, keepdims=True)
+        place = lax.broadcasted_iota(jnp.int32, (capacity, rows), 0).astype(f32)
+        return (place == pos_e) & (has_e > 0.5)
+
+    def as_bf(mask):
+        return mask.astype(f32).astype(bf)
 
     pl.semaphore_wait(barrier, owners + splits - 1)
 
@@ -205,7 +210,7 @@
     for i in steps:
         rt(i).start()
     for i in steps:
-        x_send[i] = jnp.dot(picks(rt_recv[0], line(i)[0]), tokens_ref[...], preferred_element_type=f32).astype(bf)
+        x_send[i] = jnp.dot(as_bf(picks(0, line(i)[0])), tokens_ref[...], preferred_element_type=f32).astype(bf)
         send_x(i).start()
 
     my_half = pl.ds(pl.multiple_of(r * half, half), half)
@@ -226,7 +231,7 @@
         far(cot_ref.at[my_half], z, False).start()
 
     cots[z] = cot_ref[...]
-    x_recv[0] = jnp.dot(picks(rt_recv[0], z), tokens_ref[...], preferred_element_type=f32).astype(bf)
+    x_recv[0] = jnp.dot(as_bf(picks(0, z)), tokens_ref[...], preferred_element_type=f32).astype(bf)
 
     def pass_on(d):
         @pl.when(z - d >= 0)
@@ -263,8 +268,9 @@
             part[d, p, 0:capacity] = jnp.dot(x, gate_w[:, slices(p)], preferred_element_type=f32).astype(bf)
             part[d, p, capacity:2 * capacity] = jnp.dot(x, up_w[:, slices(p)], preferred_element_type=f32).astype(bf)
 
-    def back(d):
-        rows_in = jnp.dot(picks(rt_recv[d], z), cots[source_at(d)], preferred_element_type=f32).astype(bf)
+    def back(i, d):
+        pick = pair_picks[i, 0:capacity]
+        rows_in = jnp.dot(pick, cots[source_at(d)], preferred_element_type=f32).astype(bf)
         for p in range(splits):
             part[d, p, 2 * capacity:3 * capacity] = lax.dot_general(
                 rows_in, down_w[slices(p), :], (((1,), (1,)), ((), ())), preferred_element_type=f32
@@ -284,13 +290,41 @@
     def gg(d, q):
         return remote(grads.at[d, c], grads.at[d, c], gg_ssem.at[d, q], gg_rsem.at[d, q], ctx=peer_at(q))
 
-    def out(i):
+    own, landed = pl.ds(0, capacity), pl.ds(capacity, capacity)
+
+    def to_partner(k, i):
+        at = 0 if i == 1 else i
+        return remote(stack.at[k, i, own], stack.at[k, at, landed], pair_ssem.at[k, i], pair_rsem.at[k, at], exp=partner)
+
+    def landed_at(k, at):
+        return remote(stack.at[k, at, own], stack.at[k, at, landed], pair_ssem.at[k, at], pair_rsem.at[k, at], exp=partner)
+
+    def to_source(k, i):
+        return remote(sums.at[k, i - 2], sum_recv.at[k], sum_ssem.at[k, i - 2], sum_rsem.at[k], exp=line(i)[0])
+
+    def hand_on(k, i):
+        if i == 1:
+            to_partner(k, i).start()
+        elif i > 1:
+            @pl.when(~inner)
+            def _():
+                to_partner(k, i).start()
+
+    step = 256 if columns % 256 == 0 else columns
+
+    def relay(k, i):
+        @pl.when(inner)
+        def _():
+            landed_at(k, i).wait_recv()
+            for n in range(0, columns, step):
+                sums[k, i - 2, :, n:n + step] = lax.dot_general(
+                    pair_picks[i], stack[k, i, :, n:n + step], (((0,), (0,)), ((), ())), preferred_element_type=f32
+                ).astype(bf)
+            to_source(k, i).start()
+
+    def wgz(i):
         other, d, _ = line(i)
-        return remote(out_send.at[i], out_recv.at[d], out_ssem.at[i], out_rsem.at[d], exp=other)
-
-    def eg(i):
-        other, d, _ = line(i)
-        return remote(eg_send.at[i], eg_recv.at[d], eg_ssem.at[i], eg_rsem.at[d], exp=other)
+        return remote(wg_send.at[i], wg_recv.at[d], wgz_ssem.at[i], wgz_rsem.at[d], exp=other)
 
     others = range(1, splits)
 
@@ -311,13 +345,20 @@
         if i > 0:
             other, d, _ = line(i)
             sibling(other).wait_recv()
-        back(d)
+        back(i, d)
         for q in others:
             bk(d, q).start()
 
     def first_block(i):
         d = got_x(i) if i else 0
         first(d)
+        mine = picks(d, z)
+        pair_picks[i, 0:capacity] = as_bf(mine)
+        if i != 1:
+            pair_picks[i, capacity:] = as_bf(picks(d, partner))
+        expert = z.astype(f32)
+        named = jnp.where(rt_recv[d, 0:2] == expert, rt_recv[d, 2:4], 0.0)
+        slot_w[i] = jnp.sum(jnp.where(mine, jnp.sum(named, axis=0, keepdims=True), 0.0), axis=1, keepdims=True)
         for q in others:
             rs(d, q).start()
 
@@ -329,12 +370,15 @@
         for q in others:
             ag(d, q).wait_recv()
         act = jnp.concatenate([acts[d, p] for p in range(splits)], axis=1)
-        target = out_send if i else out_recv
-        target[i] = jnp.dot(act, down_w[...], preferred_element_type=f32).astype(bf)
-        if i:
-            out(i).start()
-
-    def grad_block(d):
+        weight = slot_w[i]
+        for n in range(0, columns, step):
+            stack[0, i, 0:capacity, n:n + step] = (
+                weight * jnp.dot(act, down_w[:, n:n + step], preferred_element_type=f32)
+            ).astype(bf)
+        hand_on(0, i)
+
+    def grad_block(i):
+        d = slot(i)
         for q in others:
             bk(d, q).wait_recv()
         back_pre = part[d, c, 2 * capacity:].astype(f32)
@@ -342,6 +386,13 @@
             back_pre = back_pre + shares[d, q, 2 * capacity:].astype(f32)
         gate_pre, up_pre = saved[d, 0:capacity], saved[d, capacity:]
         squash = jax.nn.sigmoid(gate_pre)
+        per_slot = jnp.sum(acts[d, c].astype(f32) * back_pre, axis=1, keepdims=True)
+        per_token = jnp.sum(jnp.where(pair_picks[i, 0:capacity].astype(f32) > 0.5, per_slot, 0.0), axis=0, keepdims=True)
+        where_to = wg_send if i else wg_recv
+        where_to[i] = jnp.broadcast_to(per_token, (8, rows))
+        if i:
+            wgz(i).start()
+        back_pre = slot_w[i] * back_pre
         grads[d, c, 0:capacity] = (back_pre * up_pre * squash * (1.0 + gate_pre * (1.0 - squash))).astype(bf)
         grads[d, c, capacity:] = (back_pre * gate_pre * squash).astype(bf)
         for q in others:
@@ -351,103 +402,88 @@
         d = slot(i)
         for q in others:
             gg(d, q).wait_recv()
-        target = eg_send if i else eg_recv
         gate_g = jnp.concatenate([grads[d, p, 0:capacity] for p in range(splits)], axis=1)
         up_g = jnp.concatenate([grads[d, p, capacity:] for p in range(splits)], axis=1)
-        step = 256 if columns % 256 == 0 else columns
         for n in range(0, columns, step):
             nt = (((1,), (1,)), ((), ()))
-            target[i, :, n:n + step] = (
+            stack[1, i, 0:capacity, n:n + step] = (
                 lax.dot_general(gate_g, gate_w[n:n + step], nt, preferred_element_type=f32)
                 + lax.dot_general(up_g, up_w[n:n + step], nt, preferred_element_type=f32)
             ).astype(bf)
-        if i:
-            eg(i).start()
+        hand_on(1, i)
 
     first_block(0)
     back_block(0)
-    last = owners - 1
     for i in steps:
         first_block(i)
         activate_block(slot(i - 1))
         if i > 1:
             out_block(i - 1)
-        pass_on(i)
-    activate_block(slot(last))
-    for i in steps:
-        back_block(i)
-        if i == 1:
-            out_block(last)
+        if i < 3:
+            pass_on(i)
+    activate_block(slot(3))
+    back_block(1)
+    out_block(3)
+    pass_on(3)
+    back_block(2)
+    back_block(3)
+    relay(0, 2)
     grad_block(0)
-    for i in steps:
-        grad_block(slot(i))
-        if i > 1:
-            eg_block(i - 1)
-    eg_block(last)
+    grad_block(1)
+    relay(0, 3)
+    grad_block(2)
+    grad_block(3)
+    eg_block(2)
+    eg_block(3)
+    eg_block(1)
+    relay(1, 2)
     out_block(0)
+    relay(1, 3)
     eg_block(0)
-
-    def weight_row(expert):
-        return jnp.sum(jnp.where(routes == expert, event_w, 0.0), axis=0, keepdims=True)
-
-    def chosen(expert):
-        mine = lax.broadcasted_iota(jnp.int32, (rows, 16), 1) == expert
-        pos = jnp.sum(jnp.where(mine, places, 0.0), axis=1, keepdims=True)
-        has = jnp.sum(jnp.where(mine, named, 0.0), axis=1, keepdims=True)
-        weight = jnp.sum(jnp.where(eye, weight_row(expert), 0.0), axis=1, keepdims=True)
-        place = lax.broadcasted_iota(jnp.int32, (rows, capacity), 1).astype(f32)
-        return ((place == pos) & (has > 0.5)).astype(bf), weight
-
-    step = 256 if columns % 256 == 0 else columns
-
-    def collect(i, recv, into, with_dot):
-        expert, d = z, 0
-        if i:
-            expert, _, d = line(i)
-        pick, weight = chosen(expert)
-        dots = jnp.zeros((rows, 1), f32)
-        for n in range(0, columns, step):
-            at = slice(n, n + step)
-            row = jnp.dot(pick, recv[d, :, at], preferred_element_type=f32)
-            total = weight * row
-            if i > 0:
-                total = total + mix_acc[:, at]
-            if i == last:
-                into[:, at] = total.astype(bf)
-            else:
-                mix_acc[:, at] = total
-            if with_dot:
-                dots = dots + jnp.sum(row * cot_ref[:, at].astype(f32), axis=1, keepdims=True)
-        if not with_dot:
-            return None
-        return jnp.where(routes == expert, jnp.sum(jnp.where(eye, dots, 0.0), axis=0, keepdims=True), 0.0)
 
     def wg(q):
         return remote(wg_parts.at[0], wg_parts.at[q], wg_ssem.at[q], wg_rsem.at[q], ctx=peer_at(q))
 
     acc = jnp.zeros(routes.shape, f32)
     for i in range(owners):
+        expert, _, d = line(i)
         if i:
-            remote(out_send.at[i], out_recv.at[line(i)[2]], out_ssem.at[i], out_rsem.at[line(i)[2]], exp=line(i)[0]).wait_recv()
-        acc = acc + collect(i, out_recv, mixed_ref, True)
+            remote(wg_send.at[i], wg_recv.at[d], wgz_ssem.at[i], wgz_rsem.at[d], exp=expert).wait_recv()
+        acc = acc + jnp.where(routes == expert, wg_recv[d if i else 0, 0:1], 0.0)
     wg_parts[0, 0:routes.shape[0]] = acc
     wg_parts[0, routes.shape[0]:] = jnp.zeros((8 - routes.shape[0], rows), f32)
     for q in others:
         wg(q).start()
-    for i in range(owners):
-        if i:
-            remote(eg_send.at[i], eg_recv.at[line(i)[2]], eg_ssem.at[i], eg_rsem.at[line(i)[2]], exp=line(i)[0]).wait_recv()
-        collect(i, eg_recv, grad_ref, False)
+
+    def collect(k, into):
+        landed_at(k, 0).wait_recv()
+        to_source(k, 2).wait_recv()
+        for n in range(0, columns, step):
+            at = slice(n, n + step)
+            here = lax.dot_general(pair_picks[0], stack[k, 0, :, at], (((0,), (0,)), ((), ())), preferred_element_type=f32)
+            into[:, at] = (here + sum_recv[k, :, at].astype(f32)).astype(bf)
+
+    collect(0, mixed_ref)
     for q in others:
         wg(q).wait_recv()
         acc = acc + wg_parts[q, 0:routes.shape[0]]
     wgrad_ref[...] = acc
+    collect(1, grad_ref)
 
     for i in steps:
         send_x(i).wait_send()
         rt(i).wait_send()
-        out(i).wait_send()
-        eg(i).wait_send()
+        wgz(i).wait_send()
+    for k in range(2):
+        to_partner(k, 1).wait_send()
+        for i in (2, 3):
+            @pl.when(inner)
+            def _():
+                to_source(k, i).wait_send()
+
+            @pl.when(~inner)
+            def _():
+                to_partner(k, i).wait_send()
     for q in others:
         wg(q).wait_send()
         for d in range(owners):
@@ -513,21 +549,21 @@
         scratch_shapes=[
             vmem((columns, hidden), bf), vmem((columns, hidden), bf), vmem((hidden, columns), bf),
             vmem((owners, capacity, columns), bf), vmem((owners, capacity, columns), bf),
-            vmem((owners, 16, rows), bf),
+            vmem((owners, 8, rows), f32),
             vmem((owners, rows, columns), bf),
             vmem((owners, splits, 3 * capacity, part_f), bf),
             vmem((owners, splits, 3 * capacity, part_f), bf),
             vmem((owners, splits, capacity, part_f), bf),
             vmem((owners, splits, 2 * capacity, part_f), bf),
             vmem((owners, 2 * capacity, part_f), f32),
-            vmem((owners, capacity, columns), bf), vmem((owners, capacity, columns), bf),
-            vmem((owners, capacity, columns), bf), vmem((owners, capacity, columns), bf),
-            vmem((splits, 8, rows), f32),
-            vmem((rows, columns), f32),
+            vmem((2, owners, 2 * capacity, columns), bf),
+            vmem((2, 2, rows, columns), bf), vmem((2, rows, columns), bf),
+            vmem((owners, 2 * capacity, rows), bf), vmem((owners, capacity, 1), f32),
+            vmem((owners, 8, rows), f32), vmem((owners, 8, rows), f32), vmem((splits, 8, rows), f32),
             dma((3,)), per_block, per_block, per_block, per_block,
             per_block, per_block, per_block, per_block, per_block,
             per_pair, per_pair, per_pair, per_pair, per_pair, per_pair, per_pair, per_pair,
-            per_block, per_block, per_block, per_block, dma((splits,)), dma((splits,)),
+            dma((2, owners)), dma((2, owners)), dma((2, 2)), dma((2,)), per_block, per_block, dma((splits,)), dma((splits,)),
         ],
         compiler_params=pltpu.CompilerParams(
             collective_id=0, has_side_effects=True, vmem_limit_bytes=56 * 1024 * 1024
@@ -553,7 +589,7 @@
     capacity = max(2, 5 * rows * fanout // (4 * experts))
     columns = depth // splits
     return (
-        experts == owners and 1 < owners <= 8 and splits > 1 and cores == 2 and fanout == 2
+        experts == owners and owners == 4 and splits > 1 and cores == 2 and fanout == 2
         and rows == 128 and capacity % 16 == 0 and columns % 128 == 0 and hidden % (128 * splits) == 0
         and 6 * columns * hidden <= 16 * 1024 * 1024
     )

time: 105 us -> 113 us (1.076)
  Pallas kernels: 103 us -> 112 us
    pallas_call x1, Pallas kernels: 101 us -> 110 us  [shards_fused(): pl.pallas_call(functools.partial(fused, sizes), out_shape=(jax.ShapeDtype...]
where the time goes in v3:
time: 113 us; the launch traced here: 112 us
  Pallas kernels  112 us (99%)
    pallas_call x1, Pallas kernels, shards_fused(): pl.pallas_call(functools.partial(fused, sizes), out_shape=(jax.ShapeDtype...  110 us

profile of v3, /device:TPU:0, one launch (start us, length us, event | category | flops | bytes accessed | tf_op | source)
XLA Modules:
  0.0 112.4 jit_solution(15897208621389972044)
XLA Ops:
  0.6 109.6 %shard_map.94 = (bf16[128,1792]{1,0:T(8,128)(2,1)}, bf16[128,1792]{1,0:T(8,128)(2,1)}, f32[2,128]{1,0:T(2,128)}) custom-call(s32[2,128]{1,0:T(2,128)} %bitcast.3, f32[2,128]{1,0:T(2,128)} %bitcast.4, bf16[128,1792]{1,0:T(8,128)(2,1)} %tokens_ref.1, bf16[128,1792]{1,0:T(8,128)(2,1)} %cot_ref.1, bf16[1,1792,1024]{2,1,0:T(8,128)(2,1)} %gate_hbm.1, ...), custom_call_target="tpu_custom_call" | custom-call | flops 7046430720 | bytes 11010048 | tf_op jit(solution)/shard_map/pallas_call | solution.py:540
  110.3 2.1 %shard_map.95 = (bf16[128,1792]{1,0:T(8,128)(2,1)}, bf16[128,1792]{1,0:T(8,128)(2,1)}, f32[2,128]{1,0:T(2,128)}) custom-call(bf16[128,1792]{1,0:T(8,128)(2,1)} %get-tuple-element.9.refs_0_, bf16[128,1792]{1,0:T(8,128)(2,1)} %get-tuple-element.10.refs_1_, f32[2,128]{1,0:T(2,128)} %get-tuple-element.11.refs_2_), custom_call_target="tpu_custom_call" | custom-call | bytes 1835008 | tf_op jit(solution)/shard_map/pallas_call | solution.py:575

commit v4 on v3

--- a/solution.py
+++ b/solution.py
@@ -113,10 +113,10 @@
     routes_ref, weights_ref, tokens_ref, cot_ref, gate_hbm, up_hbm, down_hbm,
     mixed_ref, grad_ref, wgrad_ref,
     gate_w, up_w, down_w, x_send, x_recv, rt_recv, cots, part, shares, acts, grads, saved,
-    stack, sums, sum_recv, pair_picks, slot_w, wg_send, wg_recv, wg_parts,
+    stack, far_rows, sums, sum_recv, pair_picks, slot_w, wg_send, wg_recv, wg_parts,
     load_sem, x_ssem, x_rsem, rt_ssem, rt_rsem, far_up, far_down, far_rsem, sib_ssem, sib_rsem,
     rs_ssem, rs_rsem, bk_ssem, bk_rsem, ag_ssem, ag_rsem, gg_ssem, gg_rsem,
-    pair_ssem, pair_rsem, sum_ssem, sum_rsem, wgz_ssem, wgz_rsem, wg_ssem, wg_rsem,
+    pair_ssem, pair_rsem, direct_ssem, direct_rsem, sum_ssem, sum_rsem, wgz_ssem, wgz_rsem, wg_ssem, wg_rsem,
 ):
     owners, splits, capacity, rows, columns, hidden = sizes
     part_f = hidden // splits
@@ -186,6 +186,9 @@
         place = lax.broadcasted_iota(jnp.int32, (capacity, rows), 0).astype(f32)
         return (place == pos_e) & (has_e > 0.5)
 
+    def slot(i):
+        return line(i)[1] if i else 0
+
     def as_bf(mask):
         return mask.astype(f32).astype(bf)
 
@@ -222,13 +225,14 @@
     def sibling(j):
         return remote(cots.at[j, my_half], cots.at[j, my_half], sib_ssem.at[j], sib_rsem.at[j], rep=1 - r)
 
-    @pl.when(z < owners - 1)
-    def _():
-        far(cot_ref.at[my_half], z, True).start()
-
-    @pl.when(z > 0)
-    def _():
-        far(cot_ref.at[my_half], z, False).start()
+    def start_cots():
+        @pl.when(z < owners - 1)
+        def _():
+            far(cot_ref.at[my_half], z, True).start()
+
+        @pl.when(z > 0)
+        def _():
+            far(cot_ref.at[my_half], z, False).start()
 
     cots[z] = cot_ref[...]
     x_recv[0] = jnp.dot(as_bf(picks(0, z)), tokens_ref[...], preferred_element_type=f32).astype(bf)
@@ -262,19 +266,26 @@
     def slices(p):
         return slice(p * part_f, (p + 1) * part_f)
 
-    def first(d):
-        x = x_recv[d]
+    def first(pair):
+        x = jnp.concatenate([x_recv[slot(i)] for i in pair], axis=0)
         for p in range(splits):
-            part[d, p, 0:capacity] = jnp.dot(x, gate_w[:, slices(p)], preferred_element_type=f32).astype(bf)
-            part[d, p, capacity:2 * capacity] = jnp.dot(x, up_w[:, slices(p)], preferred_element_type=f32).astype(bf)
-
-    def back(i, d):
-        pick = pair_picks[i, 0:capacity]
-        rows_in = jnp.dot(pick, cots[source_at(d)], preferred_element_type=f32).astype(bf)
+            gate = jnp.dot(x, gate_w[:, slices(p)], preferred_element_type=f32).astype(bf)
+            up = jnp.dot(x, up_w[:, slices(p)], preferred_element_type=f32).astype(bf)
+            for n, i in enumerate(pair):
+                part[slot(i), p, 0:capacity] = gate[n * capacity:(n + 1) * capacity]
+                part[slot(i), p, capacity:2 * capacity] = up[n * capacity:(n + 1) * capacity]
+
+    def back(pair):
+        rows_in = jnp.concatenate([
+            jnp.dot(pair_picks[i, 0:capacity], cots[source_at(slot(i))], preferred_element_type=f32).astype(bf)
+            for i in pair
+        ], axis=0)
         for p in range(splits):
-            part[d, p, 2 * capacity:3 * capacity] = lax.dot_general(
+            got = lax.dot_general(
                 rows_in, down_w[slices(p), :], (((1,), (1,)), ((), ())), preferred_element_type=f32
             ).astype(bf)
+            for n, i in enumerate(pair):
+                part[slot(i), p, 2 * capacity:3 * capacity] = got[n * capacity:(n + 1) * capacity]
 
     def rs(d, q):
         at = pl.ds(0, 2 * capacity)
@@ -302,9 +313,19 @@
     def to_source(k, i):
         return remote(sums.at[k, i - 2], sum_recv.at[k], sum_ssem.at[k, i - 2], sum_rsem.at[k], exp=line(i)[0])
 
+    def direct(i):
+        at = pl.ds(pl.multiple_of(jnp.where(inner, 0, capacity), capacity), capacity)
+        return remote(stack.at[0, i, own], far_rows.at[at], direct_ssem.at[i - 2], direct_rsem.at[jnp.where(inner, 0, 1)], exp=line(i)[0])
+
+    def got_direct(n):
+        at = pl.ds(n * capacity, capacity)
+        return remote(stack.at[0, 2 + n, own], far_rows.at[at], direct_ssem.at[n], direct_rsem.at[n], exp=line(2 + n)[0])
+
     def hand_on(k, i):
         if i == 1:
             to_partner(k, i).start()
+        elif i > 1 and k == 0:
+            direct(i).start()
         elif i > 1:
             @pl.when(~inner)
             def _():
@@ -340,42 +361,46 @@
         for q in others:
             ag(d, q).start()
 
-    def back_block(i):
-        d = 0
-        if i > 0:
-            other, d, _ = line(i)
-            sibling(other).wait_recv()
-        back(i, d)
-        for q in others:
-            bk(d, q).start()
-
-    def first_block(i):
-        d = got_x(i) if i else 0
-        first(d)
+    def back_blocks(pair):
+        for i in pair:
+            if i:
+                sibling(line(i)[0]).wait_recv()
+        back(pair)
+        for i in pair:
+            for q in others:
+                bk(slot(i), q).start()
+
+    def pick_block(i):
+        d = slot(i)
         mine = picks(d, z)
         pair_picks[i, 0:capacity] = as_bf(mine)
         if i != 1:
             pair_picks[i, capacity:] = as_bf(picks(d, partner))
         expert = z.astype(f32)
-        named = jnp.where(rt_recv[d, 0:2] == expert, rt_recv[d, 2:4], 0.0)
-        slot_w[i] = jnp.sum(jnp.where(mine, jnp.sum(named, axis=0, keepdims=True), 0.0), axis=1, keepdims=True)
-        for q in others:
-            rs(d, q).start()
-
-    def slot(i):
-        return line(i)[1] if i else 0
-
-    def out_block(i):
-        d = slot(i)
-        for q in others:
-            ag(d, q).wait_recv()
-        act = jnp.concatenate([acts[d, p] for p in range(splits)], axis=1)
-        weight = slot_w[i]
+        weights = jnp.where(rt_recv[d, 0:2] == expert, rt_recv[d, 2:4], 0.0)
+        slot_w[i] = jnp.sum(jnp.where(mine, jnp.sum(weights, axis=0, keepdims=True), 0.0), axis=1, keepdims=True)
+
+    def first_blocks(pair):
+        first(pair)
+        for i in pair:
+            for q in others:
+                rs(slot(i), q).start()
+        for i in pair:
+            pick_block(i)
+
+    def out_blocks(pair):
+        for i in pair:
+            for q in others:
+                ag(slot(i), q).wait_recv()
+        act = jnp.concatenate([
+            jnp.concatenate([acts[slot(i), p] for p in range(splits)], axis=1) for i in pair
+        ], axis=0)
         for n in range(0, columns, step):
-            stack[0, i, 0:capacity, n:n + step] = (
-                weight * jnp.dot(act, down_w[:, n:n + step], preferred_element_type=f32)
-            ).astype(bf)
-        hand_on(0, i)
+            got = jnp.dot(act, down_w[:, n:n + step], preferred_element_type=f32)
+            for m, i in enumerate(pair):
+                stack[0, i, 0:capacity, n:n + step] = (slot_w[i] * got[m * capacity:(m + 1) * capacity]).astype(bf)
+        for i in pair:
+            hand_on(0, i)
 
     def grad_block(i):
         d = slot(i)
@@ -398,48 +423,51 @@
         for q in others:
             gg(d, q).start()
 
-    def eg_block(i):
-        d = slot(i)
-        for q in others:
-            gg(d, q).wait_recv()
-        gate_g = jnp.concatenate([grads[d, p, 0:capacity] for p in range(splits)], axis=1)
-        up_g = jnp.concatenate([grads[d, p, capacity:] for p in range(splits)], axis=1)
+    def eg_blocks(pair):
+        for i in pair:
+            for q in others:
+                gg(slot(i), q).wait_recv()
+        gate_g = jnp.concatenate([
+            jnp.concatenate([grads[slot(i), p, 0:capacity] for p in range(splits)], axis=1) for i in pair
+        ], axis=0)
+        up_g = jnp.concatenate([
+            jnp.concatenate([grads[slot(i), p, capacity:] for p in range(splits)], axis=1) for i in pair
+        ], axis=0)
+        nt = (((1,), (1,)), ((), ()))
         for n in range(0, columns, step):
-            nt = (((1,), (1,)), ((), ()))
-            stack[1, i, 0:capacity, n:n + step] = (
+            got = (
                 lax.dot_general(gate_g, gate_w[n:n + step], nt, preferred_element_type=f32)
                 + lax.dot_general(up_g, up_w[n:n + step], nt, preferred_element_type=f32)
             ).astype(bf)
-        hand_on(1, i)
-
-    first_block(0)
-    back_block(0)
-    for i in steps:
-        first_block(i)
-        activate_block(slot(i - 1))
-        if i > 1:
-            out_block(i - 1)
-        if i < 3:
-            pass_on(i)
+            for m, i in enumerate(pair):
+                stack[1, i, 0:capacity, n:n + step] = got[m * capacity:(m + 1) * capacity]
+        for i in pair:
+            hand_on(1, i)
+
+    near, distant = (0, 1), (2, 3)
+    got_x(1)
+    first_blocks(near)
+    activate_block(slot(0))
+    activate_block(slot(1))
+    got_x(2)
+    start_cots()
+    got_x(3)
+    first_blocks(distant)
+    out_blocks(near)
+    pass_on(1)
+    activate_block(slot(2))
     activate_block(slot(3))
-    back_block(1)
-    out_block(3)
+    back_blocks(near)
+    out_blocks(distant)
+    pass_on(2)
     pass_on(3)
-    back_block(2)
-    back_block(3)
-    relay(0, 2)
-    grad_block(0)
-    grad_block(1)
-    relay(0, 3)
-    grad_block(2)
-    grad_block(3)
-    eg_block(2)
-    eg_block(3)
-    eg_block(1)
+    back_blocks(distant)
+    for i in range(owners):
+        grad_block(i)
+    eg_blocks(distant)
+    eg_blocks(near)
     relay(1, 2)
-    out_block(0)
     relay(1, 3)
-    eg_block(0)
 
     def wg(q):
         return remote(wg_parts.at[0], wg_parts.at[q], wg_ssem.at[q], wg_rsem.at[q], ctx=peer_at(q))
@@ -455,35 +483,44 @@
     for q in others:
         wg(q).start()
 
-    def collect(k, into):
-        landed_at(k, 0).wait_recv()
-        to_source(k, 2).wait_recv()
-        for n in range(0, columns, step):
-            at = slice(n, n + step)
-            here = lax.dot_general(pair_picks[0], stack[k, 0, :, at], (((0,), (0,)), ((), ())), preferred_element_type=f32)
-            into[:, at] = (here + sum_recv[k, :, at].astype(f32)).astype(bf)
-
-    collect(0, mixed_ref)
+    tn = (((0,), (0,)), ((), ()))
+    far_picks = jnp.concatenate([as_bf(picks(0, line(2)[0])), as_bf(picks(0, line(3)[0]))], axis=0)
+    landed_at(0, 0).wait_recv()
+    got_direct(0).wait_recv()
+    got_direct(1).wait_recv()
+    for n in range(0, columns, step):
+        at = slice(n, n + step)
+        mixed_ref[:, at] = (
+            lax.dot_general(pair_picks[0], stack[0, 0, :, at], tn, preferred_element_type=f32)
+            + lax.dot_general(far_picks, far_rows[:, at], tn, preferred_element_type=f32)
+        ).astype(bf)
     for q in others:
         wg(q).wait_recv()
         acc = acc + wg_parts[q, 0:routes.shape[0]]
     wgrad_ref[...] = acc
-    collect(1, grad_ref)
+    landed_at(1, 0).wait_recv()
+    to_source(1, 2).wait_recv()
+    for n in range(0, columns, step):
+        at = slice(n, n + step)
+        here = lax.dot_general(pair_picks[0], stack[1, 0, :, at], tn, preferred_element_type=f32)
+        grad_ref[:, at] = (here + sum_recv[1, :, at].astype(f32)).astype(bf)
 
     for i in steps:
         send_x(i).wait_send()
         rt(i).wait_send()
         wgz(i).wait_send()
-    for k in range(2):
-        to_partner(k, 1).wait_send()
-        for i in (2, 3):
-            @pl.when(inner)
-            def _():
-                to_source(k, i).wait_send()
-
-            @pl.when(~inner)
-            def _():
-                to_partner(k, i).wait_send()
+    to_partner(0, 1).wait_send()
+    to_partner(1, 1).wait_send()
+    for i in (2, 3):
+        direct(i).wait_send()
+
+        @pl.when(inner)
+        def _():
+            to_source(1, i).wait_send()
+
+        @pl.when(~inner)
+        def _():
+            to_partner(1, i).wait_send()
     for q in others:
         wg(q).wait_send()
         for d in range(owners):
@@ -557,13 +594,13 @@
             vmem((owners, splits, 2 * capacity, part_f), bf),
             vmem((owners, 2 * capacity, part_f), f32),
             vmem((2, owners, 2 * capacity, columns), bf),
-            vmem((2, 2, rows, columns), bf), vmem((2, rows, columns), bf),
+            vmem((2 * capacity, columns), bf), vmem((2, 2, rows, columns), bf), vmem((2, rows, columns), bf),
             vmem((owners, 2 * capacity, rows), bf), vmem((owners, capacity, 1), f32),
             vmem((owners, 8, rows), f32), vmem((owners, 8, rows), f32), vmem((splits, 8, rows), f32),
             dma((3,)), per_block, per_block, per_block, per_block,
             per_block, per_block, per_block, per_block, per_block,
             per_pair, per_pair, per_pair, per_pair, per_pair, per_pair, per_pair, per_pair,
-            dma((2, owners)), dma((2, owners)), dma((2, 2)), dma((2,)), per_block, per_block, dma((splits,)), dma((splits,)),
+            dma((2, owners)), dma((2, owners)), dma((2,)), dma((2,)), dma((2, 2)), dma((2,)), per_block, per_block, dma((splits,)), dma((splits,)),
         ],
         compiler_params=pltpu.CompilerParams(
             collective_id=0, has_side_effects=True, vmem_limit_bytes=56 * 1024 * 1024

time: 113 us -> 120 us (1.062)
  Pallas kernels: 112 us -> 119 us
    pallas_call x1, Pallas kernels: 110 us -> 117 us  [shards_fused(): pl.pallas_call(functools.partial(fused, sizes), out_shape=(jax.ShapeDtype...]
where the time goes in v4:
time: 120 us
  Pallas kernels  119 us (99%)
    pallas_call x1, Pallas kernels, shards_fused(): pl.pallas_call(functools.partial(fused, sizes), out_shape=(jax.ShapeDtype...  117 us

profile of v4, /device:TPU:0, one launch (start us, length us, event | category | flops | bytes accessed | tf_op | source)
XLA Modules:
  0.0 120.0 jit_solution(6441541298898210212)
XLA Ops:
  0.6 117.2 %shard_map.94 = (bf16[128,1792]{1,0:T(8,128)(2,1)}, bf16[128,1792]{1,0:T(8,128)(2,1)}, f32[2,128]{1,0:T(2,128)}) custom-call(s32[2,128]{1,0:T(2,128)} %bitcast.3, f32[2,128]{1,0:T(2,128)} %bitcast.4, bf16[128,1792]{1,0:T(8,128)(2,1)} %tokens_ref.1, bf16[128,1792]{1,0:T(8,128)(2,1)} %cot_ref.1, bf16[1,1792,1024]{2,1,0:T(8,128)(2,1)} %gate_hbm.1, ...), custom_call_target="tpu_custom_call" | custom-call | flops 7046430720 | bytes 11010048 | tf_op jit(solution)/shard_map/pallas_call | solution.py:577
  117.8 2.1 %shard_map.95 = (bf16[128,1792]{1,0:T(8,128)(2,1)}, bf16[128,1792]{1,0:T(8,128)(2,1)}, f32[2,128]{1,0:T(2,128)}) custom-call(bf16[128,1792]{1,0:T(8,128)(2,1)} %get-tuple-element.9.refs_0_, bf16[128,1792]{1,0:T(8,128)(2,1)} %get-tuple-element.10.refs_1_, f32[2,128]{1,0:T(2,128)} %get-tuple-element.11.refs_2_), custom_call_target="tpu_custom_call" | custom-call | bytes 1835008 | tf_op jit(solution)/shard_map/pallas_call | solution.py:612

commit v5 on v3

--- a/solution.py
+++ b/solution.py
@@ -113,10 +113,10 @@
     routes_ref, weights_ref, tokens_ref, cot_ref, gate_hbm, up_hbm, down_hbm,
     mixed_ref, grad_ref, wgrad_ref,
     gate_w, up_w, down_w, x_send, x_recv, rt_recv, cots, part, shares, acts, grads, saved,
-    stack, sums, sum_recv, pair_picks, slot_w, wg_send, wg_recv, wg_parts,
+    stack, landing, all_picks, pair_picks, slot_w, wg_send, wg_recv, wg_parts,
     load_sem, x_ssem, x_rsem, rt_ssem, rt_rsem, far_up, far_down, far_rsem, sib_ssem, sib_rsem,
     rs_ssem, rs_rsem, bk_ssem, bk_rsem, ag_ssem, ag_rsem, gg_ssem, gg_rsem,
-    pair_ssem, pair_rsem, sum_ssem, sum_rsem, wgz_ssem, wgz_rsem, wg_ssem, wg_rsem,
+    res_ssem, res_rsem, wgz_ssem, wgz_rsem, wg_ssem, wg_rsem,
 ):
     owners, splits, capacity, rows, columns, hidden = sizes
     part_f = hidden // splits
@@ -269,7 +269,7 @@
             part[d, p, capacity:2 * capacity] = jnp.dot(x, up_w[:, slices(p)], preferred_element_type=f32).astype(bf)
 
     def back(i, d):
-        pick = pair_picks[i, 0:capacity]
+        pick = pair_picks[i]
         rows_in = jnp.dot(pick, cots[source_at(d)], preferred_element_type=f32).astype(bf)
         for p in range(splits):
             part[d, p, 2 * capacity:3 * capacity] = lax.dot_general(
@@ -290,37 +290,21 @@
     def gg(d, q):
         return remote(grads.at[d, c], grads.at[d, c], gg_ssem.at[d, q], gg_rsem.at[d, q], ctx=peer_at(q))
 
-    own, landed = pl.ds(0, capacity), pl.ds(capacity, capacity)
-
-    def to_partner(k, i):
-        at = 0 if i == 1 else i
-        return remote(stack.at[k, i, own], stack.at[k, at, landed], pair_ssem.at[k, i], pair_rsem.at[k, at], exp=partner)
-
-    def landed_at(k, at):
-        return remote(stack.at[k, at, own], stack.at[k, at, landed], pair_ssem.at[k, at], pair_rsem.at[k, at], exp=partner)
-
-    def to_source(k, i):
-        return remote(sums.at[k, i - 2], sum_recv.at[k], sum_ssem.at[k, i - 2], sum_rsem.at[k], exp=line(i)[0])
+    def result(k, i):
+        other, d, _ = line(i)
+        at = pl.ds(pl.multiple_of(d * capacity, capacity), capacity)
+        return remote(stack.at[k, i], landing.at[k, at], res_ssem.at[k, i], res_rsem.at[k, d], exp=other)
+
+    def got_result(k, i):
+        other, _, d = line(i)
+        at = pl.ds(pl.multiple_of(d * capacity, capacity), capacity)
+        return remote(stack.at[k, i], landing.at[k, at], res_ssem.at[k, i], res_rsem.at[k, d], exp=other)
 
     def hand_on(k, i):
-        if i == 1:
-            to_partner(k, i).start()
-        elif i > 1:
-            @pl.when(~inner)
-            def _():
-                to_partner(k, i).start()
+        if i:
+            result(k, i).start()
 
     step = 256 if columns % 256 == 0 else columns
-
-    def relay(k, i):
-        @pl.when(inner)
-        def _():
-            landed_at(k, i).wait_recv()
-            for n in range(0, columns, step):
-                sums[k, i - 2, :, n:n + step] = lax.dot_general(
-                    pair_picks[i], stack[k, i, :, n:n + step], (((0,), (0,)), ((), ())), preferred_element_type=f32
-                ).astype(bf)
-            to_source(k, i).start()
 
     def wgz(i):
         other, d, _ = line(i)
@@ -353,9 +337,7 @@
         d = got_x(i) if i else 0
         first(d)
         mine = picks(d, z)
-        pair_picks[i, 0:capacity] = as_bf(mine)
-        if i != 1:
-            pair_picks[i, capacity:] = as_bf(picks(d, partner))
+        pair_picks[i] = as_bf(mine)
         expert = z.astype(f32)
         named = jnp.where(rt_recv[d, 0:2] == expert, rt_recv[d, 2:4], 0.0)
         slot_w[i] = jnp.sum(jnp.where(mine, jnp.sum(named, axis=0, keepdims=True), 0.0), axis=1, keepdims=True)
@@ -372,7 +354,8 @@
         act = jnp.concatenate([acts[d, p] for p in range(splits)], axis=1)
         weight = slot_w[i]
         for n in range(0, columns, step):
-            stack[0, i, 0:capacity, n:n + step] = (
+            into = stack.at[0, i] if i else landing.at[0, 0:capacity]
+            into[:, n:n + step] = (
                 weight * jnp.dot(act, down_w[:, n:n + step], preferred_element_type=f32)
             ).astype(bf)
         hand_on(0, i)
@@ -387,7 +370,7 @@
         gate_pre, up_pre = saved[d, 0:capacity], saved[d, capacity:]
         squash = jax.nn.sigmoid(gate_pre)
         per_slot = jnp.sum(acts[d, c].astype(f32) * back_pre, axis=1, keepdims=True)
-        per_token = jnp.sum(jnp.where(pair_picks[i, 0:capacity].astype(f32) > 0.5, per_slot, 0.0), axis=0, keepdims=True)
+        per_token = jnp.sum(jnp.where(pair_picks[i].astype(f32) > 0.5, per_slot, 0.0), axis=0, keepdims=True)
         where_to = wg_send if i else wg_recv
         where_to[i] = jnp.broadcast_to(per_token, (8, rows))
         if i:
@@ -406,7 +389,8 @@
         up_g = jnp.concatenate([grads[d, p, capacity:] for p in range(splits)], axis=1)
         for n in range(0, columns, step):
             nt = (((1,), (1,)), ((), ()))
-            stack[1, i, 0:capacity, n:n + step] = (
+            into = stack.at[1, i] if i else landing.at[1, 0:capacity]
+            into[:, n:n + step] = (
                 lax.dot_general(gate_g, gate_w[n:n + step], nt, preferred_element_type=f32)
                 + lax.dot_general(up_g, up_w[n:n + step], nt, preferred_element_type=f32)
             ).astype(bf)
@@ -414,31 +398,32 @@
 
     first_block(0)
     back_block(0)
-    for i in steps:
-        first_block(i)
-        activate_block(slot(i - 1))
-        if i > 1:
-            out_block(i - 1)
-        if i < 3:
-            pass_on(i)
+    for d in range(owners):
+        all_picks[:, d * capacity:(d + 1) * capacity] = as_bf(picks(0, expert_at(d))).astype(f32).T.astype(bf)
+    first_block(1)
+    activate_block(slot(0))
+    pass_on(1)
+    first_block(2)
+    activate_block(slot(1))
+    out_block(1)
+    first_block(3)
+    activate_block(slot(2))
+    pass_on(2)
+    out_block(2)
+    back_block(1)
     activate_block(slot(3))
-    back_block(1)
     out_block(3)
+    grad_block(0)
+    grad_block(1)
     pass_on(3)
     back_block(2)
     back_block(3)
-    relay(0, 2)
-    grad_block(0)
-    grad_block(1)
-    relay(0, 3)
+    eg_block(1)
     grad_block(2)
     grad_block(3)
     eg_block(2)
     eg_block(3)
-    eg_block(1)
-    relay(1, 2)
     out_block(0)
-    relay(1, 3)
     eg_block(0)
 
     def wg(q):
@@ -456,12 +441,11 @@
         wg(q).start()
 
     def collect(k, into):
-        landed_at(k, 0).wait_recv()
-        to_source(k, 2).wait_recv()
+        for i in steps:
+            got_result(k, i).wait_recv()
         for n in range(0, columns, step):
             at = slice(n, n + step)
-            here = lax.dot_general(pair_picks[0], stack[k, 0, :, at], (((0,), (0,)), ((), ())), preferred_element_type=f32)
-            into[:, at] = (here + sum_recv[k, :, at].astype(f32)).astype(bf)
+            into[:, at] = jnp.dot(all_picks[...], landing[k, :, at], preferred_element_type=f32).astype(bf)
 
     collect(0, mixed_ref)
     for q in others:
@@ -474,16 +458,8 @@
         send_x(i).wait_send()
         rt(i).wait_send()
         wgz(i).wait_send()
-    for k in range(2):
-        to_partner(k, 1).wait_send()
-        for i in (2, 3):
-            @pl.when(inner)
-            def _():
-                to_source(k, i).wait_send()
-
-            @pl.when(~inner)
-            def _():
-                to_partner(k, i).wait_send()
+        for k in range(2):
+            result(k, i).wait_send()
     for q in others:
         wg(q).wait_send()
         for d in range(owners):
@@ -556,14 +532,14 @@
             vmem((owners, splits, capacity, part_f), bf),
             vmem((owners, splits, 2 * capacity, part_f), bf),
             vmem((owners, 2 * capacity, part_f), f32),
-            vmem((2, owners, 2 * capacity, columns), bf),
-            vmem((2, 2, rows, columns), bf), vmem((2, rows, columns), bf),
-            vmem((owners, 2 * capacity, rows), bf), vmem((owners, capacity, 1), f32),
+            vmem((2, owners, capacity, columns), bf), vmem((2, owners * capacity, columns), bf),
+            vmem((rows, owners * capacity), bf),
+            vmem((owners, capacity, rows), bf), vmem((owners, capacity, 1), f32),
             vmem((owners, 8, rows), f32), vmem((owners, 8, rows), f32), vmem((splits, 8, rows), f32),
             dma((3,)), per_block, per_block, per_block, per_block,
             per_block, per_block, per_block, per_block, per_block,
             per_pair, per_pair, per_pair, per_pair, per_pair, per_pair, per_pair, per_pair,
-            dma((2, owners)), dma((2, owners)), dma((2, 2)), dma((2,)), per_block, per_block, dma((splits,)), dma((splits,)),
+            dma((2, owners)), dma((2, owners)), per_block, per_block, dma((splits,)), dma((splits,)),
         ],
         compiler_params=pltpu.CompilerParams(
             collective_id=0, has_side_effects=True, vmem_limit_bytes=56 * 1024 * 1024

time: 113 us -> 106 us (0.938)
  Pallas kernels: 112 us -> 105 us
    pallas_call x1, Pallas kernels: 110 us -> 103 us  [shards_fused(): pl.pallas_call(functools.partial(fused, sizes), out_shape=(jax.ShapeDtype...]
where the time goes in v5:
time: 106 us
  Pallas kernels  105 us (99%)
    pallas_call x1, Pallas kernels, shards_fused(): pl.pallas_call(functools.partial(fused, sizes), out_shape=(jax.ShapeDtype...  103 us

profile of v5, /device:TPU:0, one launch (start us, length us, event | category | flops | bytes accessed | tf_op | source)
XLA Modules:
  0.0 106.1 jit_solution(5024375272625130120)
XLA Ops:
  0.6 103.3 %shard_map.94 = (bf16[128,1792]{1,0:T(8,128)(2,1)}, bf16[128,1792]{1,0:T(8,128)(2,1)}, f32[2,128]{1,0:T(2,128)}) custom-call(s32[2,128]{1,0:T(2,128)} %bitcast.3, f32[2,128]{1,0:T(2,128)} %bitcast.4, bf16[128,1792]{1,0:T(8,128)(2,1)} %tokens_ref.1, bf16[128,1792]{1,0:T(8,128)(2,1)} %cot_ref.1, bf16[1,1792,1024]{2,1,0:T(8,128)(2,1)} %gate_hbm.1, ...), custom_call_target="tpu_custom_call" | custom-call | flops 7046430720 | bytes 11010048 | tf_op jit(solution)/shard_map/pallas_call | solution.py:516
  104.0 2.1 %shard_map.95 = (bf16[128,1792]{1,0:T(8,128)(2,1)}, bf16[128,1792]{1,0:T(8,128)(2,1)}, f32[2,128]{1,0:T(2,128)}) custom-call(bf16[128,1792]{1,0:T(8,128)(2,1)} %get-tuple-element.9.refs_0_, bf16[128,1792]{1,0:T(8,128)(2,1)} %get-tuple-element.10.refs_1_, f32[2,128]{1,0:T(2,128)} %get-tuple-element.11.refs_2_), custom_call_target="tpu_custom_call" | custom-call | bytes 1835008 | tf_op jit(solution)/shard_map/pallas_call | solution.py:551

commit v6 on v5

--- a/solution.py
+++ b/solution.py
@@ -418,12 +418,12 @@
     pass_on(3)
     back_block(2)
     back_block(3)
-    eg_block(1)
+    out_block(0)
     grad_block(2)
     grad_block(3)
+    eg_block(1)
     eg_block(2)
     eg_block(3)
-    out_block(0)
     eg_block(0)
 
     def wg(q):
@@ -495,8 +495,12 @@
 
 
 def hand_over(*refs):
-    for source, target in zip(refs[:3], refs[3:]):
-        target[...] = source[...]
+    sems = refs[6]
+    copies = [pltpu.make_async_copy(refs[n], refs[n + 3], sems.at[n]) for n in range(3)]
+    for copy in copies:
+        copy.start()
+    for copy in copies:
+        copy.wait()
 
 
 def shards_fused(tokens, routes, event_weights, cotangent, w_gate, w_up, w_down):
@@ -551,8 +555,9 @@
     mixed, token_grad, weight_grad = pl.pallas_call(
         hand_over,
         out_shape=tuple(jax.ShapeDtypeStruct(x.shape, x.dtype) for x in results),
-        in_specs=[full] * 3,
-        out_specs=(full,) * 3,
+        in_specs=[anywhere] * 3,
+        out_specs=(anywhere,) * 3,
+        scratch_shapes=[dma((3,))],
         cost_estimate=pl.CostEstimate(flops=0, bytes_accessed=8 * rows * columns, transcendentals=0),
     )(*results)
     return mixed, token_grad, weight_grad.T

time: 106 us -> 134 us (1.26)
  Pallas kernels: 105 us -> 133 us
    pallas_call x1, Pallas kernels: 2.11 us -> 29 us  [shards_fused(): pl.pallas_call(hand_over, out_shape=tuple((jax.ShapeDtypeStruct(x.shape,...]
where the time goes in v6:
time: 134 us
  Pallas kernels  133 us (99%)
    pallas_call x1, Pallas kernels, shards_fused(): pl.pallas_call(functools.partial(fused, sizes), out_shape=(jax.ShapeDtype...  104 us
    pallas_call x1, Pallas kernels, shards_fused(): pl.pallas_call(hand_over, out_shape=tuple((jax.ShapeDtypeStruct(x.shape,...  29 us

profile of v6, /device:TPU:0, one launch (start us, length us, event | category | flops | bytes accessed | tf_op | source)
XLA Modules:
  0.0 134.0 jit_solution(9373296608495128936)
XLA Ops:
  0.6 104.2 %shard_map.94 = (bf16[128,1792]{1,0:T(8,128)(2,1)}, bf16[128,1792]{1,0:T(8,128)(2,1)}, f32[2,128]{1,0:T(2,128)}) custom-call(s32[2,128]{1,0:T(2,128)} %bitcast.3, f32[2,128]{1,0:T(2,128)} %bitcast.4, bf16[128,1792]{1,0:T(8,128)(2,1)} %tokens_ref.1, bf16[128,1792]{1,0:T(8,128)(2,1)} %cot_ref.1, bf16[1,1792,1024]{2,1,0:T(8,128)(2,1)} %gate_hbm.1, ...), custom_call_target="tpu_custom_call" | custom-call | flops 7046430720 | bytes 11010048 | tf_op jit(solution)/shard_map/pallas_call | solution.py:520
  104.9 29.0 %shard_map.95 = (bf16[128,1792]{1,0:T(8,128)(2,1)}, bf16[128,1792]{1,0:T(8,128)(2,1)}, f32[2,128]{1,0:T(2,128)}) custom-call(bf16[128,1792]{1,0:T(8,128)(2,1)} %get-tuple-element.9.refs_0_, bf16[128,1792]{1,0:T(8,128)(2,1)} %get-tuple-element.10.refs_1_, f32[2,128]{1,0:T(2,128)} %get-tuple-element.11.refs_2_), custom_call_target="tpu_custom_call" | custom-call | bytes 1835008 | tf_op jit(solution)/shard_map/pallas_call | solution.py:555
